TPU v7x, 512 devices: a whole 4x8x8 slice. The times are simulated.
512 devices in a mesh: section: 8 (over y_hi, x), dp: 64 (over y_lo, z, core).
Axes of the slice: x: 4, y: 8 (y_hi: 2, y_lo: 4; y = y_hi * 4 + y_lo), z: 8, core: 2. Of those that a mesh axis runs over, the one named last changes fastest.
Arguments:
- embeds: bfloat16 [12288, 3584], P('dp'), may hold values from -16 to 16
- cotangent: bfloat16 [12288, 3584], P('dp'), may hold values from -1 to 1
- adapter_a: bfloat16 [8, 7168, 128], P('section', 'dp'), may hold values from -0.0625 to 0.0625
- adapter_b: bfloat16 [8, 128, 3584], P('section', None, 'dp'), may hold values from -0.5 to 0.5
- norm_gains: float32 [2, 7168], replicated, may hold values from 0.5 to 1.5
Outputs:
- grad_a: float32 [8, 7168, 128], P('section', 'dp')
- grad_b: float32 [8, 128, 3584], P('section')
- grad_gain: float32 [2, 7168], P(None, 'dp')
- grad_embed: bfloat16 [12288, 3584], P('dp', 'section')
All inputs are finite; a program needn't handle non-finite values.
Results may differ from a plain program's by a relative error of at most 0.023.
Values may be sent and summed in bfloat16 or wider, within the bound.
A program may use at most 64 MiB of HBM per device.

v0:
```python
import jax
import jax.numpy as jnp
from jax import lax
from jax.sharding import PartitionSpec as P

MROWS = 24


epsilon = 1e-05


def from_behind(block, axis, distance):
    devices = range(lax.axis_size(axis))
    route = [(i - distance, i) for i in devices if i - distance in devices]
    return lax.ppermute(block, axis, route)


def normalize(hidden, embeds, gain_row):
    joined = jnp.concatenate([hidden.astype(jnp.float32), embeds.astype(jnp.float32)], axis=1)
    inv_rms = lax.rsqrt(jnp.mean(joined * joined, axis=1, keepdims=True) + epsilon)
    normed = joined * inv_rms
    lowered = (normed * gain_row[None, :]).astype(jnp.bfloat16)
    return (normed, inv_rms, lowered)


def contract(left_op, right_op, left_dim, right_dim):
    return lax.dot_general(
        left_op,
        right_op,
        (((left_dim,), (right_dim,)), ((), ())),
        preferred_element_type=jnp.float32,
    )


def pass_on(payload, offset):
    return from_behind(payload, "section", offset)


def pick(stacked, index):
    return lax.dynamic_index_in_dim(stacked, index, 0, keepdims=False)


def place(stacked, index, value, active):
    current = pick(stacked, index)
    return lax.dynamic_update_index_in_dim(stacked, jnp.where(active, value, current), index, 0)


def per_device(embeds, cotangent, adapter_a, adapter_b, norm_gains):
    sections = lax.axis_size("section")
    section_id = lax.axis_index("section")
    down_mat, up_mat = (
        lax.all_gather(adapter_a[0], "dp", axis=0, tiled=True),
        lax.all_gather(adapter_b[0], "dp", axis=1, tiled=True),
    )
    parity = section_id % 2
    gain_row = jnp.where(parity == 0, norm_gains[0], norm_gains[1])
    model_width = embeds.shape[1]
    joined_width = down_mat.shape[0]
    low_rank = down_mat.shape[1]
    group_size = 1
    block_rows = MROWS * group_size
    block_count = embeds.shape[0] // block_rows
    tick_count = block_count + sections - 1
    embed_blocks = embeds.reshape(block_count, block_rows, model_width)
    target_blocks = cotangent.reshape(block_count, block_rows, model_width)

    def forward_tick(tick, state_in):
        incoming, hidden_keep, reduced_keep = state_in
        block_index = tick - section_id
        active = (block_index >= 0) & (block_index < block_count)
        safe_index = jnp.clip(block_index, 0, block_count - 1)
        embed_block = pick(embed_blocks, safe_index)
        hidden = jnp.where(section_id == 0, embed_block, incoming)
        normed, inv_rms, lowered = normalize(hidden, embed_block, gain_row)
        reduced = jnp.dot(lowered, down_mat, preferred_element_type=jnp.float32).astype(
            jnp.bfloat16
        )
        output = (
            hidden.astype(jnp.float32)
            + jnp.dot(reduced, up_mat, preferred_element_type=jnp.float32)
        ).astype(jnp.bfloat16)
        hidden_keep = place(hidden_keep, safe_index, hidden, active)
        reduced_keep = place(reduced_keep, safe_index, reduced, active)
        outgoing = jnp.where(active, output, jnp.zeros_like(output))
        return (pass_on(outgoing, 1), hidden_keep, reduced_keep)

    forward_init = (
        jnp.zeros((block_rows, model_width), jnp.bfloat16),
        jnp.zeros((block_count, block_rows, model_width), jnp.bfloat16),
        jnp.zeros((block_count, block_rows, low_rank), jnp.bfloat16),
    )
    last_sent, hidden_keep, reduced_keep = lax.fori_loop(0, tick_count, forward_tick, forward_init)

    def backward_tick(tick, state_in):
        incoming, grad_a, grad_b, gain_acc, term_keep = state_in
        block_index = tick - (sections - 1 - section_id)
        active = (block_index >= 0) & (block_index < block_count)
        safe_index = jnp.clip(block_index, 0, block_count - 1)
        target = pick(target_blocks, safe_index)
        back_in = jnp.where(section_id == sections - 1, target, incoming)
        back_in = jnp.where(active, back_in, jnp.zeros_like(back_in))
        hidden = pick(hidden_keep, safe_index)
        reduced = pick(reduced_keep, safe_index)
        embed_block = pick(embed_blocks, safe_index)
        normed, inv_rms, lowered = normalize(hidden, embed_block, gain_row)
        up_grad = contract(back_in, up_mat, 1, 1).astype(jnp.bfloat16)
        grad_b = grad_b + contract(reduced, back_in, 0, 0)
        grad_lowered = contract(up_grad, down_mat, 1, 1)
        grad_a = grad_a + contract(lowered, up_grad, 0, 0)
        gain_acc = gain_acc + jnp.sum(grad_lowered * normed, axis=0)
        scaled = grad_lowered * gain_row[None, :]
        grad_joined = inv_rms * (scaled - normed * jnp.mean(scaled * normed, axis=1, keepdims=True))
        back_out = (back_in.astype(jnp.float32) + grad_joined[:, :model_width]).astype(jnp.bfloat16)
        embed_tail = grad_joined[:, model_width:] + jnp.where(
            section_id == 0, back_out.astype(jnp.float32), 0.0
        )
        term_keep = place(term_keep, safe_index, embed_tail.astype(jnp.bfloat16), active)
        return (pass_on(back_out, -1), grad_a, grad_b, gain_acc, term_keep)

    backward_init = (
        jnp.zeros((block_rows, model_width), jnp.bfloat16),
        jnp.zeros((joined_width, low_rank), jnp.float32),
        jnp.zeros((low_rank, model_width), jnp.float32),
        jnp.zeros((joined_width,), jnp.float32),
        jnp.zeros((block_count, block_rows, model_width), jnp.bfloat16),
    )
    last_back, grad_a, grad_b, gain_acc, term_keep = lax.fori_loop(
        0, tick_count, backward_tick, backward_init
    )
    gain_pair = jnp.stack(
        [jnp.where(parity == 0, gain_acc, 0.0), jnp.where(parity == 1, gain_acc, 0.0)]
    )
    grad_a_part, gain_part = (
        lax.psum_scatter(grad_a, "dp", scatter_dimension=0, tiled=True),
        lax.psum_scatter(gain_pair, "dp", scatter_dimension=1, tiled=True),
    )
    grad_b_sum = lax.psum(grad_b, "dp")
    embed_terms = term_keep.reshape(-1, model_width).astype(jnp.float32)
    embed_sum, gain_sum = (
        lax.psum(embed_terms.astype(jnp.bfloat16), "section").astype(jnp.float32),
        lax.psum(gain_part.astype(jnp.bfloat16), "section").astype(jnp.float32),
    )
    column_count = model_width // sections
    embed_cols = lax.dynamic_slice_in_dim(embed_sum, section_id * column_count, column_count, 1)
    return (grad_a_part[None], grad_b_sum[None], gain_sum, embed_cols.astype(jnp.bfloat16))


def solution(mesh):
    in_specs = (
        P("dp", None),
        P("dp", None),
        P("section", "dp", None),
        P("section", None, "dp"),
        P(),
    )
    out_specs = (
        P("section", "dp", None),
        P("section", None, None),
        P(None, "dp"),
        P("dp", "section"),
    )
    return jax.shard_map(
        per_device, mesh=mesh, in_specs=in_specs, out_specs=out_specs, check_vma=False
    )
```

profile of v0, /device:TPU:4, one launch (start us, length us, event | category | flops | bytes accessed | tf_op | source)
XLA Modules:
  0.0 1952.0 jit_solution(14938094379765959038)
XLA Ops:
  8.0 88.8 %all-gather.1 = bf16[1,128,3584]{1,2,0:T(8,128)(2,1)S(1)} all-gather(bf16[1,128,56]{1,2,0:T(8,128)(2,1)} %param.12), channel_id=3, replica_groups=mesh['section'=8,'dp'=64] {'dp'}, dimensions={2}, use_global_device_ids=true | all-gather | bytes 931840 | tf_op jit(solution)/shard_map/all_gather | solution.py:53
  97.4 34.4 %all-gather.4.cloned.1.call-done = bf16[1,7168,128]{2,1,0:T(8,128)(2,1)} async-done(((bf16[1,112,128]{2,1,0:T(8,128)(2,1)}), bf16[1,7168,128]{2,1,0:T(8,128)(2,1)}) %all-gather.4.cloned.1.call-update) | async-done | bytes 1835024 | tf_op jit(solution)/shard_map/all_gather | solution.py:52
  133.7 266.8 %while.42 = (s32[]{:T(128)}, bf16[24,3584]{1,0:T(8,128)(2,1)S(1)}, bf16[8,24,3584]{2,1,0:T(8,128)(2,1)}, bf16[8,24,128]{2,1,0:T(8,128)(2,1)}, s32[]{:T(128)}, /*...) while((s32[]{:T(128)}, bf16[24,3584]{1,0:T(8,128)(2,1)S(1)}, ...), condition=%wide.region_2.3_spmd, body=%wide.region_0.2_spmd.sunk | while | flops 67958816 | bytes 14632085 | solution.py:92
  166.2 10.4 collective-permute-start
  184.5 10.5 collective-permute-start
  202.9 10.4 collective-permute-start
  221.2 10.4 collective-permute-start
  239.5 10.5 collective-permute-start
  257.9 10.5 collective-permute-start
  276.3 10.5 collective-permute-start
  294.7 10.5 collective-permute-start
  313.1 10.5 collective-permute-start
  331.5 10.5 collective-permute-start
  349.9 10.5 collective-permute-start
  368.3 10.5 collective-permute-start
  386.9 10.6 collective-permute-start
  402.3 307.5 %while.43 = (s32[]{:T(128)}, bf16[24,3584]{1,0:T(8,128)(2,1)}, f32[7168,128]{1,0:T(8,128)}, f32[128,3584]{1,0:T(8,128)}, f32[7168]{0:T(1024)S(1)}, /*index=5*/bf...) while((s32[]{:T(128)}, bf16[24,3584]{1,0:T(8,128)(2,1)}, ...), condition=%wide.region_7.8_spmd.clone, body=%wide.region_3.7_spmd.clone.sunk | while | flops 141248544 | bytes 44095332 | solution.py:127
  414.2 8.1 collective-permute-done.1
  436.9 8.2 collective-permute-done.1
  714.3 290.3 %reduce-scatter.7.cloned.1.call-done = f32[112,2]{1,0:T(8,128)} async-done(((f32[7168,2]{1,0:T(8,128)}), f32[112,2]{1,0:T(8,128)}) %reduce-scatter.7.cloned.1.call-update) | async-done | bytes 912
  1005.5 21.8 %psum.22 = bf16[2,112]{1,0:T(2,128)(2,1)S(1)} all-reduce(bf16[2,112]{1,0:T(2,128)(2,1)S(1)} %copy.13), channel_id=1, replica_groups=mesh['section'=8,'dp'=64] {'section'}, use_global_device_ids=true, to_apply=%region_11.12 | all-reduce | flops 224 | bytes 896 | tf_op jit(solution)/shard_map/psum | solution.py:141
  1027.9 91.5 %all-reduce.5.cloned.1.call-done = bf16[192,3584]{1,0:T(8,128)(2,1)} async-done(((bf16[192,3584]{1,0:T(8,128)(2,1)}), bf16[192,3584]{1,0:T(8,128)(2,1)}) %all-reduce.5.cloned.1.call-update) | async-done | bytes 1376272 | tf_op jit(solution)/shard_map/psum | solution.py:140
  1121.1 535.4 %all-reduce.3.cloned.1.call-done = f32[1,128,3584]{2,1,0:T(8,128)} async-done(((f32[1,128,3584]{2,1,0:T(8,128)}), f32[1,128,3584]{2,1,0:T(8,128)}) %all-reduce.3.cloned.1.call-update) | async-done | bytes 1835024 | tf_op jit(solution)/shard_map/psum | solution.py:137
  1656.5 286.1 %reduce-scatter.5.cloned.1.call-done = f32[112,128]{1,0:T(8,128)} async-done(((f32[7168,128]{1,0:T(8,128)}), f32[112,128]{1,0:T(8,128)}) %reduce-scatter.5.cloned.1.call-update) | async-done | bytes 57360 | tf_op jit(solution)/shard_map/reduce_scatter | solution.py:134
  (539 shorter events, 435.5 us)
Async XLA Ops:
  7.2 124.6 %all-gather.4.cloned.1.call-start = ((), (), s32[]{:S(2)}) async-start(), calls=%async_computation.5 | async-start | bytes 1863680 | tf_op jit(solution)/shard_map/all_gather | solution.py:52
  7.9 996.7 %reduce-scatter.7.cloned.1.call-start = ((), (), s32[]{:S(2)}) async-start(), calls=%async_computation.6 | async-start | bytes 3727360
  184.5 13.4 collective-permute-start
  239.5 13.4 collective-permute-start
  276.3 13.4 collective-permute-start
  368.3 13.7 collective-permute-start
  386.9 13.5 collective-permute-start
  408.3 14.0 collective-permute-start.1
  428.9 16.2 collective-permute-start.1
  451.7 15.1 collective-permute-start.1
  473.4 13.6 collective-permute-start.1
  513.5 13.6 collective-permute-start.1
  533.7 13.6 collective-permute-start.1
  554.0 13.6 collective-permute-start.1
  574.2 13.6 collective-permute-start.1
  594.4 13.6 collective-permute-start.1
  614.6 13.6 collective-permute-start.1
  634.9 13.6 collective-permute-start.1
  655.1 13.6 collective-permute-start.1
  675.3 13.6 collective-permute-start.1
  695.6 13.6 collective-permute-start.1
  712.4 407.0 %all-reduce.5.cloned.1.call-start = ((), (), s32[]{:S(2)}) async-start(), calls=%async_computation.4 | async-start | bytes 2752512 | tf_op jit(solution)/shard_map/psum | solution.py:140
  713.1 943.4 %all-reduce.3.cloned.1.call-start = ((), (), s32[]{:S(2)}) async-start(), calls=%async_computation.3 | async-start | bytes 3670016 | tf_op jit(solution)/shard_map/psum | solution.py:137
  713.7 1228.9 %reduce-scatter.5.cloned.1.call-start = ((), (), s32[]{:S(2)}) async-start(), calls=%async_computation.2 | async-start | bytes 3727360 | tf_op jit(solution)/shard_map/reduce_scatter | solution.py:134
  (87 other events, 508.1 us)
Sparse Core Ops, SparseCore 0:
  10.2 121.5 all-gather.3
  712.5 292.0 reduce-scatter.6
  1007.8 111.5 all-reduce.4
  1122.7 533.7 all-reduce.2
  1660.0 282.5 reduce-scatter.4
where the time goes:
time: 1960 us; the launch traced here: 1950 us
  waiting for transfers between devices  1380 us (70%)
  starting transfers between devices  174 us (9%)
  matrix products  132 us (7%)
  blocking collectives  111 us (6%)
  local copies, waits for them, and re-layouts  78.5 us (4%)
  other arithmetic  64.9 us (3%)
    psum x1, waiting for transfers between devices, per_device(): grad_b_sum = lax.psum(grad_b, 'dp')  535 us
    unnamed x6, waiting for transfers between devices  293 us
    reduce_scatter x1, waiting for transfers between devices, per_device(): lax.psum_scatter(grad_a, 'dp', scatter_dimension=0, tiled=True)  286 us
    ppermute x30, starting transfers between devices, from_behind(): return lax.ppermute(block, axis, route)  174 us
    ppermute x30, waiting for transfers between devices, from_behind(): return lax.ppermute(block, axis, route)  136 us
    dot_general x60, matrix products, contract(): lax.dot_general(left_op, right_op, (((left_dim,), (right_dim,)), ((), ())...  112 us
    psum x1, waiting for transfers between devices, per_device(): lax.psum(embed_terms.astype(jnp.bfloat16), 'section').astype(jnp.float32)  91.5 us
    all_gather x1, blocking collectives, per_device(): lax.all_gather(adapter_b[0], 'dp', axis=1, tiled=True)  88.8 us
  transfers between devices with their start and end apart: 35, of which 35 were waited for; matrix products, arithmetic and copies ran while one was open for 5% of the time, Pallas kernels for 0%

commit v1 on v0

v1 whole, which is shorter than its diff:
```python
import functools

import jax
import jax.numpy as jnp
from jax import lax
from jax.experimental import pallas as pl
from jax.experimental.pallas import tpu as pltpu
from jax.sharding import PartitionSpec as P

EPS = 1e-05
CALLS = 8
DP = (4, 8, 2)
SEC = (2, 4)
BF = jnp.bfloat16
F32 = jnp.float32
MESH = pl.DeviceIdType.MESH
NT = (((1,), (1,)), ((), ()))


def start_barrier(peers):
    sem = pltpu.get_barrier_semaphore()
    for peer in peers:
        pl.semaphore_signal(sem, inc=1, device_id=peer, device_id_type=MESH)
    pl.semaphore_wait(sem, len(peers))


def remote(src, dst, send, recv, peer):
    return pltpu.make_async_remote_copy(
        src_ref=src, dst_ref=dst, send_sem=send, recv_sem=recv, device_id=peer, device_id_type=MESH
    )


def dp_place(dims):
    _, zs, cs = dims
    me = lax.axis_index("dp")
    return me // (zs * cs), lax.rem(me // cs, zs), lax.rem(me, cs)


def dp_peer(dims, y, z, c):
    _, zs, cs = dims
    return {"dp": (y * zs + z) * cs + c}


def hops(zs, stream, ys):
    long_way, short_way = zs // 2, zs - 1 - zs // 2
    return (long_way, short_way) if stream < ys // 2 else (short_way, long_way)


def gather_dp_kernel(dims, x_ref, out_ref, local_sem, ysend, yrecv, zsend, zrecv, csend, crecv):
    ys, zs, cs = dims
    y0, z0, c0 = dp_place(dims)
    right, left = lax.rem(z0 + 1, zs), lax.rem(z0 + zs - 1, zs)
    sides = (right, left)
    peers = [dp_peer(dims, lax.rem(y0 + j, ys), z0, c0) for j in range(1, ys)]
    peers += [dp_peer(dims, y0, right, c0), dp_peer(dims, y0, left, c0)]
    sibling = dp_peer(dims, y0, z0, 1 - c0)
    start_barrier(peers + [sibling])

    own = pltpu.make_async_copy(x_ref, out_ref.at[y0, z0, c0], local_sem)
    own.start()
    sent = []
    for j in range(1, ys):
        copy = remote(x_ref, out_ref.at[y0, z0, c0], ysend.at[j], yrecv.at[j], peers[j - 1])
        copy.start()
        sent.append(copy)
    own.wait()
    rows = [lax.rem(y0 + ys - j, ys) for j in range(ys)]

    def origin(side, k):
        return lax.rem(z0 + zs - k, zs) if side == 0 else lax.rem(z0 + k, zs)

    def share(j, z, index):
        block = out_ref.at[rows[j], z, c0]
        copy = remote(block, block, csend.at[j, index], crecv.at[j, index], sibling)
        copy.start()
        sent.append(copy)

    def relay(j, side, k):
        block = out_ref.at[rows[j], origin(side, k), c0]
        copy = remote(
            block, block, zsend.at[side, j, k], zrecv.at[side, j, k], dp_peer(dims, y0, sides[side], c0)
        )
        copy.start()
        sent.append(copy)

    for j in range(ys):
        if j:
            block = out_ref.at[rows[j], z0, c0]
            remote(block, block, ysend.at[j], yrecv.at[j], peers[j - 1]).wait_recv()
        for side in range(2):
            if hops(zs, j, ys)[side]:
                relay(j, side, 0)
        share(j, z0, 0)
    for k in range(1, zs // 2 + 1):
        for j in range(ys):
            for side in range(2):
                count = hops(zs, j, ys)[side]
                if k <= count:
                    block = out_ref.at[rows[j], origin(side, k), c0]
                    remote(
                        block,
                        block,
                        zsend.at[side, j, k - 1],
                        zrecv.at[side, j, k - 1],
                        dp_peer(dims, y0, sides[side], c0),
                    ).wait_recv()
                    if k < count:
                        relay(j, side, k)
                    share(j, origin(side, k), zs - k if side == 0 else k)
    for j in range(ys):
        for index in range(zs):
            block = out_ref.at[rows[j], lax.rem(z0 + index, zs), 1 - c0]
            remote(block, block, csend.at[j, index], crecv.at[j, index], sibling).wait_recv()
    for copy in sent:
        copy.wait_send()


def gather_dp(x, collective_id, dims=DP):
    ys, zs, cs = dims
    dma = pltpu.SemaphoreType.DMA
    return pl.pallas_call(
        functools.partial(gather_dp_kernel, dims),
        out_shape=jax.ShapeDtypeStruct(dims + x.shape, x.dtype),
        in_specs=[pl.BlockSpec(memory_space=pl.ANY)],
        out_specs=pl.BlockSpec(memory_space=pl.ANY),
        scratch_shapes=[
            dma,
            dma((ys,)),
            dma((ys,)),
            dma((2, ys, zs // 2)),
            dma((2, ys, zs // 2)),
            dma((ys, zs)),
            dma((ys, zs)),
        ],
        compiler_params=pltpu.CompilerParams(collective_id=collective_id, has_side_effects=True),
    )(x)


def sec_place(secs):
    me = lax.axis_index("section")
    return me // secs[1], lax.rem(me, secs[1])


def gather_sec_kernel(secs, x_ref, out_ref, local_sem, ysend, yrecv, xsend, xrecv):
    width = secs[1]
    y0, x0 = sec_place(secs)
    across = {"section": (1 - y0) * width + x0}
    beside = [{"section": y0 * width + lax.rem(x0 + j, width)} for j in range(1, width)]
    start_barrier([across] + beside)
    own = pltpu.make_async_copy(x_ref, out_ref.at[y0, x0], local_sem)
    own.start()
    sent = [remote(x_ref, out_ref.at[y0, x0], ysend, yrecv, across)]
    sent[0].start()
    for j in range(1, width):
        copy = remote(x_ref, out_ref.at[y0, x0], xsend.at[0, j], xrecv.at[0, j], beside[j - 1])
        copy.start()
        sent.append(copy)
    block = out_ref.at[1 - y0, x0]
    remote(block, block, ysend, yrecv, across).wait_recv()
    for j in range(1, width):
        copy = remote(block, block, xsend.at[1, j], xrecv.at[1, j], beside[j - 1])
        copy.start()
        sent.append(copy)
    for h in range(2):
        for j in range(1, width):
            row = y0 if h == 0 else 1 - y0
            landed = out_ref.at[row, lax.rem(x0 + width - j, width)]
            remote(landed, landed, xsend.at[h, j], xrecv.at[h, j], beside[j - 1]).wait_recv()
    own.wait()
    for copy in sent:
        copy.wait_send()


def gather_sec(x, collective_id, secs=SEC):
    dma = pltpu.SemaphoreType.DMA
    return pl.pallas_call(
        functools.partial(gather_sec_kernel, secs),
        out_shape=jax.ShapeDtypeStruct(secs + x.shape, x.dtype),
        in_specs=[pl.BlockSpec(memory_space=pl.ANY)],
        out_specs=pl.BlockSpec(memory_space=pl.ANY),
        scratch_shapes=[dma, dma, dma, dma((2, secs[1])), dma((2, secs[1]))],
        compiler_params=pltpu.CompilerParams(collective_id=collective_id, has_side_effects=True),
    )(x)


def sum_sec_kernel(count, x_ref, out_ref, landing, send1, recv1, send2, recv2):
    me = lax.axis_index("section")
    peers = [{"section": lax.rem(me + j, count)} for j in range(1, count)]
    start_barrier(peers)
    sent = []
    for j in range(1, count):
        copy = remote(
            x_ref.at[lax.rem(me + j, count)], landing.at[me], send1.at[j], recv1.at[j], peers[j - 1]
        )
        copy.start()
        sent.append(copy)
    total = x_ref[me].astype(F32)
    for j in range(1, count):
        source = lax.rem(me + count - j, count)
        block = landing.at[source]
        remote(block, block, send1.at[j], recv1.at[j], peers[j - 1]).wait_recv()
        total = total + landing[source].astype(F32)
    out_ref[me] = total.astype(out_ref.dtype)
    for j in range(1, count):
        block = out_ref.at[me]
        copy = remote(block, block, send2.at[j], recv2.at[j], peers[j - 1])
        copy.start()
        sent.append(copy)
    for j in range(1, count):
        block = out_ref.at[lax.rem(me + count - j, count)]
        remote(block, block, send2.at[j], recv2.at[j], peers[j - 1]).wait_recv()
    for copy in sent:
        copy.wait_send()


def sum_sec(x, collective_id):
    count = x.shape[0]
    dma = pltpu.SemaphoreType.DMA
    return pl.pallas_call(
        functools.partial(sum_sec_kernel, count),
        out_shape=jax.ShapeDtypeStruct(x.shape, x.dtype),
        in_specs=[pl.BlockSpec(memory_space=pltpu.VMEM)],
        out_specs=pl.BlockSpec(memory_space=pltpu.VMEM),
        scratch_shapes=[pltpu.VMEM(x.shape, x.dtype), dma((count,)), dma((count,)), dma((count,)), dma((count,))],
        compiler_params=pltpu.CompilerParams(collective_id=collective_id, has_side_effects=True),
    )(x)


def scatter_dp_kernel(
    dims, x_ref, out_ref, from_core, moving, landing, rest, from_row, csend, crecv, zsend, zrecv, ysend, yrecv
):
    ys, zs, cs = dims
    y0, z0, c0 = dp_place(dims)
    right, left = lax.rem(z0 + 1, zs), lax.rem(z0 + zs - 1, zs)
    sides = (dp_peer(dims, y0, right, c0), dp_peer(dims, y0, left, c0))
    rows = [dp_peer(dims, lax.rem(y0 + j, ys), z0, c0) for j in range(1, ys)]
    sibling = dp_peer(dims, y0, z0, 1 - c0)
    start_barrier(list(sides) + rows + [sibling])
    sent = []


    order = []
    for reach in range(zs // 2, -1, -1):
        for offset in {reach, (zs - reach) % zs}:
            order.append(offset)
    order = sorted(set(order), key=lambda o: -min(o, zs - o))
    for offset in order:
        z = lax.rem(z0 + offset, zs)
        copy = remote(
            x_ref.at[:, z, 1 - c0], from_core.at[offset], csend.at[offset], crecv.at[offset], sibling
        )
        copy.start()
        sent.append(copy)

    def core_sum(offset, j):
        z = lax.rem(z0 + offset, zs)
        return x_ref[j, z, c0].astype(F32) + from_core[offset, j].astype(F32)

    ready = set()

    def need(offset):
        if offset not in ready:
            ready.add(offset)
            block = from_core.at[offset]
            remote(block, block, csend.at[offset], crecv.at[offset], sibling).wait_recv()

    totals = {}
    for k in range(zs // 2 + 1):
        for j in range(ys):
            for side in range(2):
                count = hops(zs, j, ys)[side]
                step = k - (zs // 2 - count)
                if step < 0 or step > count:
                    continue
                reach = count - step
                offset = reach if side == 0 else (zs - reach) % zs
                if step:
                    block = landing.at[side, j, step - 1]
                    remote(
                        block, block, zsend.at[side, j, step - 1], zrecv.at[side, j, step - 1], sides[side]
                    ).wait_recv()
                    got = landing[side, j, step - 1].astype(F32)
                if reach:
                    need(offset)
                    value = core_sum(offset, j)
                    if step:
                        value = value + got
                    moving[side, j, step] = value.astype(moving.dtype)
                    copy = remote(
                        moving.at[side, j, step],
                        landing.at[side, j, step],
                        zsend.at[side, j, step],
                        zrecv.at[side, j, step],
                        sides[side],
                    )
                    copy.start()
                    sent.append(copy)
                else:
                    if j not in totals:
                        need(0)
                        totals[j] = core_sum(0, j) + got
                    else:
                        rest[j] = (totals[j] + got).astype(rest.dtype)
    own = jnp.zeros(out_ref.shape, F32)
    for i in range(1, ys):
        row = lax.rem(y0 + i, ys)
        copy = remote(rest.at[row], from_row.at[i], ysend.at[i], yrecv.at[i], rows[i - 1])
        copy.start()
        sent.append(copy)
    own = rest[y0].astype(F32)
    for i in range(1, ys):
        block = from_row.at[i]
        remote(block, block, ysend.at[i], yrecv.at[i], rows[i - 1]).wait_recv()
        own = own + from_row[i].astype(F32)
    out_ref[...] = own
    for copy in sent:
        copy.wait_send()


def scatter_dp(x, collective_id, dims=DP):
    ys, zs, cs = dims
    block = x.shape[1:]
    x = x.reshape(dims + block)
    dma = pltpu.SemaphoreType.DMA
    half = zs // 2
    return pl.pallas_call(
        functools.partial(scatter_dp_kernel, dims),
        out_shape=jax.ShapeDtypeStruct(block, F32),
        in_specs=[pl.BlockSpec(memory_space=pltpu.VMEM)],
        out_specs=pl.BlockSpec(memory_space=pltpu.VMEM),
        scratch_shapes=[
            pltpu.VMEM((zs, ys) + block, x.dtype),
            pltpu.VMEM((2, ys, half) + block, x.dtype),
            pltpu.VMEM((2, ys, half) + block, x.dtype),
            pltpu.VMEM((ys,) + block, x.dtype),
            pltpu.VMEM((ys,) + block, x.dtype),
            dma((zs,)),
            dma((zs,)),
            dma((2, ys, half)),
            dma((2, ys, half)),
            dma((ys,)),
            dma((ys,)),
        ],
        compiler_params=pltpu.CompilerParams(
            collective_id=collective_id, has_side_effects=True, vmem_limit_bytes=40 * 2**20
        ),
    )(x)


def dot(a, b):
    return jnp.dot(a, b, preferred_element_type=F32)


def dot_nt(a, b):
    return lax.dot_general(a, b, NT, preferred_element_type=F32)


def solve_kernel(
    proj_ref,
    e2_ref,
    gram_ref,
    et_ref,
    ct_ref,
    a1_ref,
    a2_ref,
    bt_ref,
    out_ref,
    ge_ref,
    r_ref,
    v_ref,
    w_ref,
    hb_ref,
    h_ref,
    acc_ref,
):
    tokens, rank = r_ref.shape[1:]
    cols = et_ref.shape[0]
    scale = 1.0 / (2 * cols * CALLS)

    def gram(t, block):
        return gram_ref[t, :, block].reshape(rank, rank)

    e2 = e2_ref[:, :1]
    h2 = e2
    invs = []
    for s in range(CALLS):
        pre = proj_ref[s, :, :rank].astype(F32)
        hb = proj_ref[s, :, rank : 2 * rank].astype(F32)
        for t in range(s):
            pre = pre + dot(r_ref[t], gram(t, 2 * s))
            hb = hb + dot(r_ref[t], gram(t, 2 * s + 1))
        inv = lax.rsqrt((e2 + h2) * scale + EPS)
        invs.append(inv)
        r = (pre * inv).astype(BF)
        r_ref[s] = r
        rn = dot(r, gram(s, 2 * s + 1))
        h2 = h2 + jnp.sum(r.astype(F32) * (2.0 * hb + rn), axis=1, keepdims=True)
        hb_ref[s] = hb + rn

    lane = lax.broadcasted_iota(jnp.int32, (tokens, rank), 1)
    kap = jnp.zeros((tokens, 1), F32)
    kmat = jnp.zeros((tokens, rank), F32)
    for s in reversed(range(CALLS)):
        u = proj_ref[s, :, 2 * rank :].astype(F32) - kap * hb_ref[s]
        for t in range(s + 1, CALLS):
            u = u + dot_nt(v_ref[t], gram(s, 2 * t)) + dot_nt(w_ref[t], gram(s, 2 * t + 1))
        u = u.astype(BF).astype(F32)
        r = r_ref[s].astype(F32)
        inv = invs[s]
        q = jnp.sum(u * r, axis=1, keepdims=True) * scale
        k = inv * inv * q
        v_ref[s] = (inv * u).astype(BF)
        w_ref[s] = (-kap * r).astype(BF)
        kmat = jnp.where(lane == s, k, kmat)
        kap = kap + k

    unit = (
        lax.broadcasted_iota(jnp.int32, (CALLS, rank), 0) == lax.broadcasted_iota(jnp.int32, (CALLS, rank), 1)
    ).astype(F32)
    krows = lax.dot_general(unit, kmat, NT, precision=lax.Precision.HIGHEST, preferred_element_type=F32)

    quarter, eighth = cols // 4, cols // 8
    filler = jnp.zeros((out_ref.shape[1] - quarter - eighth, rank), F32)
    h_ref[0] = et_ref[...]
    for t in range(CALLS):
        h = h_ref[t]
        top = dot(h, v_ref[t]).astype(BF)
        low = dot(et_ref[...], v_ref[t]).astype(BF)
        for j in range(4):
            out_ref[t * 4 + j, :quarter] = top[j * quarter : (j + 1) * quarter]
            out_ref[CALLS * 4 + t * 4 + j, :quarter] = low[j * quarter : (j + 1) * quarter]
        if t + 1 < CALLS:
            h_ref[t + 1] = (h.astype(F32) + dot_nt(bt_ref[t], r_ref[t])).astype(BF)
    back = ct_ref[...]
    acc_ref[...] = jnp.zeros(acc_ref.shape, F32)
    for t in reversed(range(CALLS)):
        part = dot(back, r_ref[t])
        for j in range(8):
            piece = jnp.concatenate([part[j * eighth : (j + 1) * eighth], filler], axis=0)
            out_ref[t * 8 + j, quarter:] = piece.astype(BF)
        krow = krows[t : t + 1]
        step = dot_nt(a1_ref[t], v_ref[t]) - krow * h_ref[t].astype(F32)
        back = (back.astype(F32) + step).astype(BF)
        acc_ref[...] += dot_nt(a2_ref[t], v_ref[t]) - krow * et_ref[...].astype(F32)
    ge_ref[...] = (acc_ref[...] + back.astype(F32)).astype(BF)


def solve(proj, e2, gram, et, ct, a1, a2, bt):
    cols, tokens = et.shape
    rank = bt.shape[-1]
    vmem = pl.BlockSpec(memory_space=pltpu.VMEM)
    return pl.pallas_call(
        solve_kernel,
        out_shape=[
            jax.ShapeDtypeStruct((64, cols // 4 + 64, rank), BF),
            jax.ShapeDtypeStruct((cols, tokens), BF),
        ],
        in_specs=[vmem] * 8,
        out_specs=[vmem] * 2,
        scratch_shapes=[
            pltpu.VMEM((CALLS, tokens, rank), BF),
            pltpu.VMEM((CALLS, tokens, rank), BF),
            pltpu.VMEM((CALLS, tokens, rank), BF),
            pltpu.VMEM((CALLS, tokens, rank), F32),
            pltpu.VMEM((CALLS, cols, tokens), BF),
            pltpu.VMEM((cols, tokens), F32),
        ],
        compiler_params=pltpu.CompilerParams(vmem_limit_bytes=48 * 2**20),
    )(proj, e2, gram, et, ct, a1, a2, bt)


def route(place):
    return [(s * 64 + d, place(s, d)) for s in range(CALLS) for d in range(64)]


def place_a(t, d):
    return (d % 32) // 4 * 64 + d // 32 * 32 + t * 4 + d % 4


def place_b(t, d):
    return d // 8 * 64 + t * 8 + d % 8


def moved(block, place, back=False):
    pairs = route(place)
    if back:
        pairs = [(b, a) for a, b in pairs]
    return lax.ppermute(block, ("section", "dp"), pairs)


def per_device(embeds, cotangent, adapter_a, adapter_b, norm_gains):
    sec = lax.axis_index("section")
    dp = lax.axis_index("dp")
    width = embeds.shape[1]
    cols = width // CALLS
    a_own = adapter_a[0]
    rank = a_own.shape[1]
    bt_own = adapter_b[0].T
    quarter, eighth = a_own.shape[0], bt_own.shape[0]
    pad = 64 - eighth
    b_pad = jnp.pad(bt_own, ((0, pad), (0, 0)))
    a_moved = moved(a_own, place_a)
    b_moved = moved(b_pad, place_b)
    sheet = gather_dp(jnp.concatenate([a_own, b_pad, a_moved, b_moved], axis=0), 0)
    sheet = sheet.reshape(64, 2 * (quarter + 64), rank)
    half = quarter + 64
    gain = jnp.where(sec % 2 == 0, norm_gains[0], norm_gains[1])
    down = sheet[:, :quarter].reshape(2, width, rank).astype(F32)
    pmat = (down[0] * gain[:width, None] + down[1] * gain[width:, None]).astype(BF)
    up = sheet[:, quarter : quarter + eighth].reshape(width, rank)
    proj = jnp.concatenate([dot(embeds, jnp.concatenate([pmat, up], axis=1)), dot(cotangent, up)], axis=1)
    proj = gather_sec(proj.astype(BF), 1).reshape(CALLS, embeds.shape[0], 3 * rank)

    gcols = lax.dynamic_slice_in_dim(norm_gains.reshape(2, 2, CALLS, cols), sec, 1, 2)[:, :, 0]
    gcalls = jnp.stack([gcols[t % 2] for t in range(CALLS)], axis=1)
    parts = sheet[:, half : half + quarter].reshape(2, CALLS, cols, rank).astype(F32)
    parts = (parts * gcalls[..., None]).astype(BF)
    bt_cols = sheet[:, half + quarter : half + quarter + eighth].reshape(CALLS, cols, rank)
    brows = lax.dynamic_index_in_dim(bt_cols, dp // 8, 0, keepdims=False)
    brows = lax.dynamic_slice_in_dim(brows, (dp % 8) * 16, 16, 1)
    both = jnp.stack([parts[0], bt_cols], axis=1)
    gpart = lax.dot_general(brows, both, (((0,), (2,)), ((), ())), preferred_element_type=F32)
    gpart = gpart.transpose(1, 2, 0, 3).reshape(CALLS, 32, rank).astype(BF)
    gram = sum_sec(gpart, 2).reshape(256, rank)
    gram = gather_dp(gram, 3).reshape(CALLS, 8, 16, 16, rank)

    esq = embeds.astype(F32)
    e2 = jnp.broadcast_to(jnp.sum(esq * esq, axis=1, keepdims=True), (embeds.shape[0], rank))
    et = lax.dynamic_slice_in_dim(embeds, sec * cols, cols, 1).T
    ct = lax.dynamic_slice_in_dim(cotangent, sec * cols, cols, 1).T
    terms, ge = solve(proj, e2, gram, et, ct, parts[0], parts[1], bt_cols)

    own = scatter_dp(terms, 4)
    w = moved(own[:quarter].astype(BF), place_a, True).astype(F32)
    gb = moved(own[quarter:].astype(BF), place_b, True)
    gain_rows = lax.dynamic_slice_in_dim(gain, dp * quarter, quarter, 0)
    grad_a = w * gain_rows[:, None]
    gain_part = jnp.sum(w * a_own.astype(F32), axis=1).astype(BF).astype(F32)
    gain_part = jnp.pad(gain_part[None], ((0, 7), (0, rank - quarter)))
    gains = gather_sec(gain_part, 5).reshape(CALLS // 2, 2, 8, rank)[:, :, 0, :quarter]
    grad_gain = jnp.sum(gains, axis=0)
    grad_b = gather_dp(gb, 6).reshape(64, 64, rank)[:, :eighth].reshape(width, rank)
    return (grad_a[None], grad_b.T.astype(F32)[None], grad_gain, ge.T)


def solution(mesh):
    in_specs = (
        P("dp", None),
        P("dp", None),
        P("section", "dp", None),
        P("section", None, "dp"),
        P(),
    )
    out_specs = (
        P("section", "dp", None),
        P("section", None, None),
        P(None, "dp"),
        P("dp", "section"),
    )
    return jax.shard_map(per_device, mesh=mesh, in_specs=in_specs, out_specs=out_specs, check_vma=False)
```

time: 1960 us -> 262 us (0.13)
  the two profiles are of different devices: /device:TPU:4 before, /device:TPU:6 now
where the time goes in v1:
time: 262 us; the launch traced here: 261 us
  Pallas kernels  201 us (77%)
  starting transfers between devices  25.3 us (10%)
  local copies, waits for them, and re-layouts  15 us (6%)
  other arithmetic  12.8 us (5%)
  waiting for transfers between devices  2.98 us (1%)
    pallas_call x3, Pallas kernels, gather_dp(): pl.pallas_call(functools.partial(gather_dp_kernel, dims), out_shape=jax.S...  106 us
    pallas_call x2, Pallas kernels, gather_sec(): pl.pallas_call(functools.partial(gather_sec_kernel, secs), out_shape=jax....  36.2 us
    pallas_call x1, Pallas kernels, scatter_dp(): pl.pallas_call(functools.partial(scatter_dp_kernel, dims), out_shape=jax....  27.8 us
    ppermute x4, starting transfers between devices, moved(): return lax.ppermute(block, ('section', 'dp'), pairs)  25.3 us
    pallas_call x1, Pallas kernels, sum_sec(): pl.pallas_call(functools.partial(sum_sec_kernel, count), out_shape=jax.Sh...  19 us
    pallas_call x1, Pallas kernels, solve(): pl.pallas_call(solve_kernel, out_shape=[jax.ShapeDtypeStruct((64, cols //...  12.5 us
    unnamed x20, local copies, waits for them, and re-layouts  7.39 us
  transfers between devices with their start and end apart: 4, of which 1 were waited for; matrix products, arithmetic and copies ran while one was open for 4% of the time, Pallas kernels for 10%

profile of v1, /device:TPU:6, one launch (start us, length us, event | category | flops | bytes accessed | tf_op | source)
XLA Modules:
  0.0 260.7 jit_solution(1112511827462180057)
XLA Ops:
  1.4 11.8 %collective-permute-start.1 = (bf16[64,128]{1,0:T(8,128)(2,1)S(1)}, bf16[64,128]{1,0:T(8,128)(2,1)S(1)}, u32[]{:S(2)}, u32[]{:S(2)}) collective-permute-start(bf16[64,128]{1,0:T(8,128)(2,1)S(1)} %pad.10), channel_id=1, source_target_pairs={{0,0},{1,1},{2,2},{3,3},{4,4},{5,5},{6,6},{7,7},{8,64},{9,65},{10,... | collective-permute-start | bytes 49160 | tf_op jit(solution)/shard_map/ppermute | solution.py:488
  13.2 1.9 collective-permute-start
  17.1 1.7 multiply_reduce_fusion
  18.8 1.2 constant_dynamic-slice_fusion.1
  20.5 3.0 %collective-permute-done = bf16[112,128]{1,0:T(8,128)(2,1)S(1)} collective-permute-done((bf16[112,128]{1,0:T(8,128)(2,1)}, bf16[112,128]{1,0:T(8,128)(2,1)S(1)}, u32[]{:S(2)}, u32[]{:S(2)}) %collective-permute-start) | collective-permute-done | bytes 28704 | tf_op jit(solution)/shard_map/ppermute | solution.py:488
  24.1 47.9 %shard_map.84 = bf16[4,8,2,352,128]{4,3,2,1,0:T(8,128)(2,1)} custom-call(bf16[352,128]{1,0:T(8,128)(2,1)} %pad_maximum_fusion.2.x_ref), custom_call_target="tpu_custom_call" | custom-call | tf_op jit(solution)/shard_map/pallas_call | solution.py:121
  72.0 1.6 fusion.27
  73.6 2.6 %fusion.26 = (bf16[64,112,128]{2,1,0:T(8,128)(2,1)S(1)}, f32[64,112,128]{2,1,0:T(8,128)S(1)}) fusion(bf16[64,352,128]{2,1,0:T(8,128)(2,1)} %bitcast.81), kind=kLoop, calls=%fused_computation.46 | loop fusion | flops 917504 | bytes 9175040 | tf_op jit(solution)/shard_map/slice | solution.py:516
  77.0 2.1 fusion.6
  80.4 21.5 %shard_map.85 = bf16[2,4,192,384]{3,2,1,0:T(8,128)(2,1)} custom-call(bf16[192,384]{1,0:T(8,128)(2,1)} %pad_maximum_fusion.1.x_ref), custom_call_target="tpu_custom_call" | custom-call | tf_op jit(solution)/shard_map/pallas_call | solution.py:176
  103.0 1.3 slice_bitcast_fusion
  105.4 19.0 %shard_map.86 = bf16[8,32,128]{2,1,0:T(8,128)(2,1)} custom-call(bf16[8,32,128]{2,1,0:T(8,128)(2,1)} %bitcast.90), custom_call_target="tpu_custom_call" | custom-call | tf_op jit(solution)/shard_map/pallas_call | solution.py:219
  124.4 32.4 %shard_map.87 = bf16[4,8,2,256,128]{4,3,2,1,0:T(8,128)(2,1)} custom-call(bf16[256,128]{1,0:T(8,128)(2,1)} %bitcast.87), custom_call_target="tpu_custom_call" | custom-call | tf_op jit(solution)/shard_map/pallas_call | solution.py:121
  158.2 12.5 %shard_map.88 = (bf16[64,176,128]{2,1,0:T(8,128)(2,1)}, bf16[448,192]{1,0:T(8,128)(2,1)S(1)}) custom-call(bf16[8,192,384]{2,1,0:T(8,128)(2,1)S(1)} %bitcast.72, f32[192,128]{1,0:T(8,128)S(1)} %broadcast_in_dim.9.e2_ref, bf16[8,8,16,16,128]{4,3,2,1,0:T(8,128)(2,1)} %bitcast.82, bf16[448,192]{1,0:T(8,128)(2,1)S(1)} %bitcast.77, bf16[448,192]{1,0:T(8,128)(2,1)S(1)} %bitcast.78, ...), custom_call_target="tpu_custom_call" | custom-call | tf_op jit(solution)/shard_map/pallas_call | solution.py:452
  170.6 1.9 copy-done.2
  172.5 27.8 %shard_map.89 = f32[176,128]{1,0:T(8,128)S(1)} custom-call(bf16[4,8,2,176,128]{4,3,2,1,0:T(8,128)(2,1)S(1)} %bitcast.76), custom_call_target="tpu_custom_call" | custom-call | tf_op jit(solution)/shard_map/pallas_call | solution.py:326
  200.4 7.4 %collective-permute-start.3 = (bf16[64,128]{1,0:T(8,128)(2,1)S(1)}, bf16[64,128]{1,0:T(8,128)(2,1)S(1)}, u32[]{:S(2)}, u32[]{:S(2)}) collective-permute-start(bf16[64,128]{1,0:T(8,128)(2,1)S(1)} %slice.104), channel_id=1, source_target_pairs={{0,0},{1,1},{2,2},{3,3},{4,4},{5,5},{6,6},{7,7},{64,8},{65,9},{66,... | collective-permute-start | bytes 49160 | tf_op jit(solution)/shard_map/ppermute | solution.py:488
  207.9 4.1 %collective-permute-start.2 = (bf16[112,128]{1,0:T(8,128)(2,1)S(1)}, bf16[112,128]{1,0:T(8,128)(2,1)S(1)}, u32[]{:S(2)}, u32[]{:S(2)}) collective-permute-start(bf16[112,128]{1,0:T(8,128)(2,1)S(1)} %slice.103), channel_id=1, source_target_pairs={{0,0},{1,1},{2,2},{3,3},{64,4},{65,5},{66,6},{67,7},{128,8},{129,9... | collective-permute-start | bytes 86024 | tf_op jit(solution)/shard_map/ppermute | solution.py:488
  212.0 1.7 copy.19
  214.3 25.7 %shard_map.90 = bf16[4,8,2,64,128]{4,3,2,1,0:T(8,128)(2,1)} custom-call(bf16[64,128]{1,0:T(8,128)(2,1)} %copy-done.7), custom_call_target="tpu_custom_call" | custom-call | tf_op jit(solution)/shard_map/pallas_call | solution.py:121
  240.0 1.3 slice.105
  241.4 1.7 copy.18
  244.5 14.8 %shard_map.91 = f32[2,4,8,128]{3,2,1,0:T(8,128)} custom-call(f32[8,128]{1,0:T(8,128)} %pad_convert_fusion.x_ref), custom_call_target="tpu_custom_call" | custom-call | tf_op jit(solution)/shard_map/pallas_call | solution.py:176
  259.3 1.3 slice_reduce_fusion.2
  (41 shorter events, 11.4 us)
Async XLA Ops:
  0.6 22.8 %copy-start.6 = (bf16[1,112,128]{2,1,0:T(8,128)(2,1)S(1)}, bf16[1,112,128]{2,1,0:T(8,128)(2,1)}, u32[]{:S(2)}) copy-start(bf16[1,112,128]{2,1,0:T(8,128)(2,1)} %param.7) | copy-start | bytes 86020
  1.4 19.1 %collective-permute-start.1 = (bf16[64,128]{1,0:T(8,128)(2,1)S(1)}, bf16[64,128]{1,0:T(8,128)(2,1)S(1)}, u32[]{:S(2)}, u32[]{:S(2)}) collective-permute-start(bf16[64,128]{1,0:T(8,128)(2,1)S(1)} %pad.10), channel_id=1, source_target_pairs={{0,0},{1,1},{2,2},{3,3},{4,4},{5,5},{6,6},{7,7},{8,64},{9,65},{10,... | collective-permute-start | bytes 49160 | tf_op jit(solution)/shard_map/ppermute | solution.py:488
  13.2 10.2 %collective-permute-start = (bf16[112,128]{1,0:T(8,128)(2,1)}, bf16[112,128]{1,0:T(8,128)(2,1)S(1)}, u32[]{:S(2)}, u32[]{:S(2)}) collective-permute-start(bf16[112,128]{1,0:T(8,128)(2,1)} %bitcast.88), channel_id=1, source_target_pairs={{0,0},{1,1},{2,2},{3,3},{4,64},{5,65},{6,66},{7,67},{8,128},{9,129... | collective-permute-start | bytes 86024 | tf_op jit(solution)/shard_map/ppermute | solution.py:488
  73.6 2.7 %copy-start.4 = (bf16[192,3584]{1,0:T(8,128)(2,1)S(1)}, bf16[192,3584]{1,0:T(8,128)(2,1)}, u32[]{:S(2)}) copy-start(bf16[192,3584]{1,0:T(8,128)(2,1)} %param.6) | copy-start | bytes 4128772
  77.0 2.2 copy-start.5
  124.4 32.5 %copy-start = (bf16[2,4,192,384]{3,2,1,0:T(8,128)(2,1)S(1)}, bf16[2,4,192,384]{3,2,1,0:T(8,128)(2,1)}, u32[]{:S(2)}) copy-start(bf16[2,4,192,384]{3,2,1,0:T(8,128)(2,1)} %shard_map.85) | copy-start | bytes 3538948
  157.0 1.2 copy-start.1
  170.6 29.7 %copy-start.3 = (bf16[448,192]{1,0:T(8,128)(2,1)}, bf16[448,192]{1,0:T(8,128)(2,1)S(1)}, u32[]{:S(2)}) copy-start(bf16[448,192]{1,0:T(8,128)(2,1)S(1)} %get-tuple-element.7) | copy-start | bytes 516100
  170.6 1.9 copy-start.2
  200.4 13.4 %collective-permute-start.3 = (bf16[64,128]{1,0:T(8,128)(2,1)S(1)}, bf16[64,128]{1,0:T(8,128)(2,1)S(1)}, u32[]{:S(2)}, u32[]{:S(2)}) collective-permute-start(bf16[64,128]{1,0:T(8,128)(2,1)S(1)} %slice.104), channel_id=1, source_target_pairs={{0,0},{1,1},{2,2},{3,3},{4,4},{5,5},{6,6},{7,7},{64,8},{65,9},{66,... | collective-permute-start | bytes 49160 | tf_op jit(solution)/shard_map/ppermute | solution.py:488
  207.9 35.2 %collective-permute-start.2 = (bf16[112,128]{1,0:T(8,128)(2,1)S(1)}, bf16[112,128]{1,0:T(8,128)(2,1)S(1)}, u32[]{:S(2)}, u32[]{:S(2)}) collective-permute-start(bf16[112,128]{1,0:T(8,128)(2,1)S(1)} %slice.103), channel_id=1, source_target_pairs={{0,0},{1,1},{2,2},{3,3},{64,4},{65,5},{66,6},{67,7},{128,8},{129,9... | collective-permute-start | bytes 86024 | tf_op jit(solution)/shard_map/ppermute | solution.py:488
  213.7 0.6 copy-start.7

commit v2 on v1

v2 whole, which is shorter than its diff:
```python
import functools

import jax
import jax.numpy as jnp
from jax import lax
from jax.experimental import pallas as pl
from jax.experimental.pallas import tpu as pltpu
from jax.sharding import PartitionSpec as P

EPS = 1e-05
CALLS = 8
DP = (4, 8, 2)
SEC = (2, 4)
BF = jnp.bfloat16
F32 = jnp.float32
MESH = pl.DeviceIdType.MESH
NT = (((1,), (1,)), ((), ()))


def start_barrier(peers, swaps=()):
    sem = pltpu.get_barrier_semaphore()
    count = len(peers)
    for peer in peers:
        pl.semaphore_signal(sem, inc=1, device_id=peer, device_id_type=MESH)
    for swap in swaps:
        swap.greet(sem)
        count = count + jnp.where(swap.stays, 0, 1)
    pl.semaphore_wait(sem, count)


def remote(src, dst, send, recv, peer):
    return pltpu.make_async_remote_copy(
        src_ref=src, dst_ref=dst, send_sem=send, recv_sem=recv, device_id=peer, device_id_type=MESH
    )


def hops(zs, stream, ys):
    long_way, short_way = zs // 2, zs - 1 - zs // 2
    return (long_way, short_way) if stream < ys // 2 else (short_way, long_way)


class Ring:
    def __init__(self, dims):
        self.dims = dims
        ys, zs, cs = dims
        me = lax.axis_index("dp")
        self.y, self.z, self.c = me // (zs * cs), lax.rem(me // cs, zs), lax.rem(me, cs)
        self.rows = [self.at(lax.rem(self.y + j, ys), self.z, self.c) for j in range(1, ys)]
        right, left = lax.rem(self.z + 1, zs), lax.rem(self.z + zs - 1, zs)
        self.sides = (self.at(self.y, right, self.c), self.at(self.y, left, self.c))
        self.sibling = self.at(self.y, self.z, 1 - self.c)
        self.peers = self.rows + list(self.sides) + [self.sibling]

    def at(self, y, z, c):
        _, zs, cs = self.dims
        return {"dp": (y * zs + z) * cs + c}


def ring_sems(dims):
    ys, zs, _ = dims
    dma = pltpu.SemaphoreType.DMA
    return [
        dma,
        dma((ys,)),
        dma((ys,)),
        dma((2, ys, zs // 2)),
        dma((2, ys, zs // 2)),
        dma((ys, zs)),
        dma((ys, zs)),
    ]


def spread(ring, src, out_ref, sems, between=None):
    local_sem, ysend, yrecv, zsend, zrecv, csend, crecv = sems
    ys, zs, cs = ring.dims
    y0, z0, c0 = ring.y, ring.z, ring.c
    own = pltpu.make_async_copy(src, out_ref.at[y0, z0, c0], local_sem)
    own.start()
    sent = []
    for j in range(1, ys):
        copy = remote(src, out_ref.at[y0, z0, c0], ysend.at[j], yrecv.at[j], ring.rows[j - 1])
        copy.start()
        sent.append(copy)
    lines = [lax.rem(y0 + ys - j, ys) for j in range(ys)]

    def origin(side, k):
        return lax.rem(z0 + zs - k, zs) if side == 0 else lax.rem(z0 + k, zs)

    def share(j, z, index):
        block = out_ref.at[lines[j], z, c0]
        copy = remote(
            block if index or j else src, block, csend.at[j, index], crecv.at[j, index], ring.sibling
        )
        copy.start()
        sent.append(copy)

    def relay(j, side, k):
        block = out_ref.at[lines[j], origin(side, k), c0]
        copy = remote(
            block if k or j else src, block, zsend.at[side, j, k], zrecv.at[side, j, k], ring.sides[side]
        )
        copy.start()
        sent.append(copy)

    for j in range(ys):
        if j:
            block = out_ref.at[lines[j], z0, c0]
            remote(block, block, ysend.at[j], yrecv.at[j], ring.rows[j - 1]).wait_recv()
        for side in range(2):
            if hops(zs, j, ys)[side]:
                relay(j, side, 0)
        share(j, z0, 0)
    if between is not None:
        between()
    for k in range(1, zs // 2 + 1):
        for j in range(ys):
            for side in range(2):
                count = hops(zs, j, ys)[side]
                if k <= count:
                    block = out_ref.at[lines[j], origin(side, k), c0]
                    remote(
                        block, block, zsend.at[side, j, k - 1], zrecv.at[side, j, k - 1], ring.sides[side]
                    ).wait_recv()
                    if k < count:
                        relay(j, side, k)
                    share(j, origin(side, k), zs - k if side == 0 else k)
    for j in range(ys):
        for index in range(zs):
            block = out_ref.at[lines[j], lax.rem(z0 + index, zs), 1 - c0]
            remote(block, block, csend.at[j, index], crecv.at[j, index], ring.sibling).wait_recv()
    own.wait()
    for copy in sent:
        copy.wait_send()


class Swap:
    def __init__(self, section, dp):
        self.peer = {"section": section, "dp": dp}
        self.stays = section == lax.axis_index("section")

    def greet(self, sem):
        @pl.when(jnp.logical_not(self.stays))
        def _():
            pl.semaphore_signal(sem, inc=1, device_id=self.peer, device_id_type=MESH)

    def start(self, src, dst, sems):
        self.local = pltpu.make_async_copy(src, dst, sems.at[0])
        self.remote = remote(src, dst, sems.at[1], sems.at[2], self.peer)

        @pl.when(self.stays)
        def _():
            self.local.start()

        @pl.when(jnp.logical_not(self.stays))
        def _():
            self.remote.start()

    def wait(self):
        @pl.when(self.stays)
        def _():
            self.local.wait()

        @pl.when(jnp.logical_not(self.stays))
        def _():
            self.remote.wait()


def swap_down(dims, count):
    size = dims[0] * dims[1] * dims[2]
    half, step = size // 2, size // 2 // count
    sec, dp = lax.axis_index("section"), lax.axis_index("dp")
    return Swap(lax.rem(dp, half) // step, dp // half * half + sec * step + lax.rem(dp, step))


def swap_up(dims, count):
    step = dims[0] * dims[1] * dims[2] // count
    sec, dp = lax.axis_index("section"), lax.axis_index("dp")
    return Swap(dp // step, sec * step + lax.rem(dp, step))


def weights_kernel(
    dims, count, a_ref, b_ref, keep_ref, give_ref, out_ref, own_ref, other_ref, hsend, hrecv, asems, bsems, *sems
):
    ring = Ring(dims)
    down, up = swap_down(dims, count), swap_up(dims, count)
    start_barrier(ring.peers, (down, up))
    rows, high = a_ref.shape[0], b_ref.shape[0]
    half = rows // 2
    down.start(a_ref, own_ref.at[pl.ds(rows, rows)], asems)
    up.start(b_ref, own_ref.at[pl.ds(2 * rows, high)], bsems)
    copy = remote(give_ref, other_ref, hsend, hrecv, ring.rows[dims[0] // 2 - 1])
    copy.start()
    copy.wait_recv()
    both = keep_ref[...].astype(F32) + other_ref[...].astype(F32)
    block = jnp.concatenate([both[:half], b_ref[...].astype(F32)[:half]], axis=0)
    own_ref[pl.ds(0, rows)] = block.astype(own_ref.dtype)
    down.wait()
    up.wait()
    spread(ring, own_ref, out_ref, sems)
    copy.wait_send()


def gather_weights(a, b, keep, give, collective_id, dims=DP, count=CALLS):
    rows = 2 * a.shape[0] + b.shape[0]
    dma = pltpu.SemaphoreType.DMA
    vmem = pl.BlockSpec(memory_space=pltpu.VMEM)
    return pl.pallas_call(
        functools.partial(weights_kernel, dims, count),
        out_shape=jax.ShapeDtypeStruct(dims + (rows, a.shape[1]), a.dtype),
        in_specs=[vmem] * 4,
        out_specs=pl.BlockSpec(memory_space=pl.ANY),
        scratch_shapes=[
            pltpu.VMEM((rows, a.shape[1]), a.dtype),
            pltpu.VMEM(give.shape, give.dtype),
            dma,
            dma,
            dma((3,)),
            dma((3,)),
        ]
        + ring_sems(dims),
        compiler_params=pltpu.CompilerParams(collective_id=collective_id, has_side_effects=True),
    )(a, b, keep, give)


def middle_kernel(
    dims,
    secs,
    gram_ref,
    proj_ref,
    gall_ref,
    pall_ref,
    landing,
    total_ref,
    send1,
    recv1,
    send2,
    recv2,
    local_sem,
    across_send,
    across_recv,
    xsend,
    xrecv,
    *sems,
):
    ring = Ring(dims)
    count, width = secs[0] * secs[1], secs[1]
    me = lax.axis_index("section")
    y0, x0 = me // width, lax.rem(me, width)
    peers = [{"section": lax.rem(me + j, count)} for j in range(1, count)]
    across = {"section": (1 - y0) * width + x0}
    beside = [{"section": y0 * width + lax.rem(x0 + j, width)} for j in range(1, width)]
    start_barrier(ring.peers + peers)
    sent = []

    def push(*what):
        copy = remote(*what)
        copy.start()
        sent.append(copy)

    for j in range(1, count):
        push(gram_ref.at[lax.rem(me + j, count)], landing.at[me], send1.at[j], recv1.at[j], peers[j - 1])
    total = gram_ref[me].astype(F32)
    for j in range(1, count):
        source = lax.rem(me + count - j, count)
        block = landing.at[source]
        remote(block, block, send1.at[j], recv1.at[j], peers[j - 1]).wait_recv()
        total = total + landing[source].astype(F32)
    total_ref[me] = total.astype(total_ref.dtype)
    for j in range(1, count):
        push(total_ref.at[me], total_ref.at[me], send2.at[j], recv2.at[j], peers[j - 1])
    own = pltpu.make_async_copy(proj_ref, pall_ref.at[y0, x0], local_sem)
    own.start()
    push(proj_ref, pall_ref.at[y0, x0], across_send, across_recv, across)
    for j in range(1, width):
        push(proj_ref, pall_ref.at[y0, x0], xsend.at[0, j], xrecv.at[0, j], beside[j - 1])
    for j in range(1, count):
        block = total_ref.at[lax.rem(me + count - j, count)]
        remote(block, block, send2.at[j], recv2.at[j], peers[j - 1]).wait_recv()

    def forward():
        block = pall_ref.at[1 - y0, x0]
        remote(block, block, across_send, across_recv, across).wait_recv()
        for j in range(1, width):
            push(block, block, xsend.at[1, j], xrecv.at[1, j], beside[j - 1])

    spread(ring, total_ref, gall_ref, sems, forward)
    for h in range(2):
        for j in range(1, width):
            landed = pall_ref.at[y0 if h == 0 else 1 - y0, lax.rem(x0 + width - j, width)]
            remote(landed, landed, xsend.at[h, j], xrecv.at[h, j], beside[j - 1]).wait_recv()
    own.wait()
    for copy in sent:
        copy.wait_send()


def gather_middle(gram, proj, collective_id, dims=DP, secs=SEC):
    dma = pltpu.SemaphoreType.DMA
    count = secs[0] * secs[1]
    anywhere = pl.BlockSpec(memory_space=pl.ANY)
    return pl.pallas_call(
        functools.partial(middle_kernel, dims, secs),
        out_shape=[
            jax.ShapeDtypeStruct(dims + gram.shape, gram.dtype),
            jax.ShapeDtypeStruct(secs + proj.shape, proj.dtype),
        ],
        in_specs=[pl.BlockSpec(memory_space=pltpu.VMEM), anywhere],
        out_specs=[anywhere, anywhere],
        scratch_shapes=[pltpu.VMEM(gram.shape, gram.dtype)] * 2
        + [dma((count,))] * 4
        + [dma, dma, dma, dma((2, secs[1])), dma((2, secs[1]))]
        + ring_sems(dims),
        compiler_params=pltpu.CompilerParams(collective_id=collective_id, has_side_effects=True),
    )(gram, proj)


def gather_sums(ring, x_ref, from_core, moving, landing, rest, from_row, csend, crecv, zsend, zrecv, ysend, yrecv):
    ys, zs, cs = ring.dims
    y0, z0, c0 = ring.y, ring.z, ring.c
    sent = []
    order = []
    for reach in range(zs // 2, -1, -1):
        for offset in {reach, (zs - reach) % zs}:
            order.append(offset)
    order = sorted(set(order), key=lambda o: -min(o, zs - o))
    for offset in order:
        z = lax.rem(z0 + offset, zs)
        copy = remote(
            x_ref.at[:, z, 1 - c0], from_core.at[offset], csend.at[offset], crecv.at[offset], ring.sibling
        )
        copy.start()
        sent.append(copy)

    def core_sum(offset, j):
        z = lax.rem(z0 + offset, zs)
        return x_ref[j, z, c0].astype(F32) + from_core[offset, j].astype(F32)

    ready = set()

    def need(offset):
        if offset not in ready:
            ready.add(offset)
            block = from_core.at[offset]
            remote(block, block, csend.at[offset], crecv.at[offset], ring.sibling).wait_recv()

    totals = {}
    for k in range(zs // 2 + 1):
        for j in range(ys):
            for side in range(2):
                count = hops(zs, j, ys)[side]
                step = k - (zs // 2 - count)
                if step < 0 or step > count:
                    continue
                reach = count - step
                offset = reach if side == 0 else (zs - reach) % zs
                if step:
                    block = landing.at[side, j, step - 1]
                    remote(
                        block, block, zsend.at[side, j, step - 1], zrecv.at[side, j, step - 1], ring.sides[side]
                    ).wait_recv()
                    got = landing[side, j, step - 1].astype(F32)
                else:
                    got = 0.0
                if reach:
                    need(offset)
                    value = core_sum(offset, j) + got
                    moving[side, j, step] = value.astype(moving.dtype)
                    copy = remote(
                        moving.at[side, j, step],
                        landing.at[side, j, step],
                        zsend.at[side, j, step],
                        zrecv.at[side, j, step],
                        ring.sides[side],
                    )
                    copy.start()
                    sent.append(copy)
                else:
                    if j not in totals:
                        need(0)
                        totals[j] = core_sum(0, j) + got
                    else:
                        rest[j] = (totals[j] + got).astype(rest.dtype)
    for i in range(1, ys):
        row = lax.rem(y0 + i, ys)
        copy = remote(rest.at[row], from_row.at[i], ysend.at[i], yrecv.at[i], ring.rows[i - 1])
        copy.start()
        sent.append(copy)
    own = rest[y0].astype(F32)
    for i in range(1, ys):
        block = from_row.at[i]
        remote(block, block, ysend.at[i], yrecv.at[i], ring.rows[i - 1]).wait_recv()
        own = own + from_row[i].astype(F32)
    return own, sent


def finish_kernel(
    dims,
    count,
    x_ref,
    a_ref,
    gain_ref,
    ga_ref,
    gb_ref,
    gg_ref,
    from_core,
    moving,
    landing,
    rest,
    from_row,
    mine,
    got,
    csend,
    crecv,
    zsend,
    zrecv,
    ysend,
    yrecv,
    asems,
    bsems,
    gsend,
    grecv,
    *sems,
):
    ring = Ring(dims)
    down, up = swap_down(dims, count), swap_up(dims, count)
    me = lax.axis_index("section")
    peers = [{"section": lax.rem(me + j, count)} for j in range(1, count)]
    start_barrier(ring.peers + peers, (down, up))
    own, sent = gather_sums(
        ring, x_ref, from_core, moving, landing, rest, from_row, csend, crecv, zsend, zrecv, ysend, yrecv
    )
    mine[...] = own.astype(mine.dtype)
    rows, rank = a_ref.shape
    high = mine.shape[0] - rows
    low_part, high_part = pl.ds(0, rows), pl.ds(rows, high)
    up.start(mine.at[high_part], got.at[high_part], bsems)
    down.start(mine.at[low_part], got.at[low_part], asems)
    up.wait()

    def gains():
        down.wait()
        w = got[low_part].astype(F32)
        ga_ref[...] = w * gain_ref[...]
        prod = w * a_ref[...].astype(F32)
        if rank > rows:
            prod = jnp.concatenate([prod, jnp.zeros((rank - rows, rank), F32)], axis=0)
        line = lax.dot_general(
            jnp.ones((8, rank), F32), prod, NT, precision=lax.Precision.HIGHEST, preferred_element_type=F32
        )
        gg_ref[me] = line.astype(BF).astype(F32)
        for j in range(1, count):
            copy = remote(gg_ref.at[me], gg_ref.at[me], gsend.at[j], grecv.at[j], peers[j - 1])
            copy.start()
            sent.append(copy)

    spread(ring, got.at[high_part], gb_ref, sems, gains)
    for j in range(1, count):
        block = gg_ref.at[lax.rem(me + count - j, count)]
        remote(block, block, gsend.at[j], grecv.at[j], peers[j - 1]).wait_recv()
    for copy in sent:
        copy.wait_send()


def finish(x, a, gain, collective_id, dims=DP, count=CALLS):
    ys, zs, cs = dims
    block = x.shape[1:]
    high = block[0] - a.shape[0]
    x = x.reshape(dims + block)
    dma = pltpu.SemaphoreType.DMA
    half = zs // 2
    vmem = pl.BlockSpec(memory_space=pltpu.VMEM)
    return pl.pallas_call(
        functools.partial(finish_kernel, dims, count),
        out_shape=[
            jax.ShapeDtypeStruct(a.shape, F32),
            jax.ShapeDtypeStruct(dims + (high, block[1]), BF),
            jax.ShapeDtypeStruct((count, 8, block[1]), F32),
        ],
        in_specs=[vmem] * 3,
        out_specs=[vmem, pl.BlockSpec(memory_space=pl.ANY), vmem],
        scratch_shapes=[
            pltpu.VMEM((zs, ys) + block, x.dtype),
            pltpu.VMEM((2, ys, half) + block, x.dtype),
            pltpu.VMEM((2, ys, half) + block, x.dtype),
            pltpu.VMEM((ys,) + block, x.dtype),
            pltpu.VMEM((ys,) + block, x.dtype),
            pltpu.VMEM(block, x.dtype),
            pltpu.VMEM(block, x.dtype),
            dma((zs,)),
            dma((zs,)),
            dma((2, ys, half)),
            dma((2, ys, half)),
            dma((ys,)),
            dma((ys,)),
            dma((3,)),
            dma((3,)),
            dma((count,)),
            dma((count,)),
        ]
        + ring_sems(dims),
        compiler_params=pltpu.CompilerParams(
            collective_id=collective_id, has_side_effects=True, vmem_limit_bytes=40 * 2**20
        ),
    )(x, a, gain)


def dot(a, b):
    return jnp.dot(a, b, preferred_element_type=F32)


def dot_nt(a, b):
    return lax.dot_general(a, b, NT, preferred_element_type=F32)


def solve_kernel(
    proj_ref,
    e2_ref,
    gram_ref,
    et_ref,
    ct_ref,
    a1_ref,
    a2_ref,
    bt_ref,
    out_ref,
    ge_ref,
    r_ref,
    v_ref,
    w_ref,
    hb_ref,
    h_ref,
    acc_ref,
):
    tokens, rank = r_ref.shape[1:]
    cols = et_ref.shape[0]
    scale = 1.0 / (2 * cols * CALLS)

    def gram(t, pos):
        return gram_ref[14 * t + pos if 2 * t < CALLS else 16 * (CALLS - 1 - t) + pos + 1]

    e2 = e2_ref[:, :1]
    h2 = e2
    invs = []
    for s in range(CALLS):
        pre = proj_ref[s, :, :rank].astype(F32)
        hb = proj_ref[s, :, rank : 2 * rank].astype(F32)
        for t in range(s):
            pre = pre + dot(r_ref[t], gram(t, 2 * s - 1))
            hb = hb + dot(r_ref[t], gram(t, 2 * s))
        inv = lax.rsqrt((e2 + h2) * scale + EPS)
        invs.append(inv)
        r = (pre * inv).astype(BF)
        r_ref[s] = r
        rn = dot(r, gram(s, 2 * s))
        h2 = h2 + jnp.sum(r.astype(F32) * (2.0 * hb + rn), axis=1, keepdims=True)
        hb_ref[s] = hb + rn

    lane = lax.broadcasted_iota(jnp.int32, (tokens, rank), 1)
    kap = jnp.zeros((tokens, 1), F32)
    kmat = jnp.zeros((tokens, rank), F32)
    for s in reversed(range(CALLS)):
        u = proj_ref[s, :, 2 * rank :].astype(F32) - kap * hb_ref[s]
        for t in range(s + 1, CALLS):
            u = u + dot_nt(v_ref[t], gram(s, 2 * t - 1)) + dot_nt(w_ref[t], gram(s, 2 * t))
        u = u.astype(BF).astype(F32)
        r = r_ref[s].astype(F32)
        inv = invs[s]
        q = jnp.sum(u * r, axis=1, keepdims=True) * scale
        k = inv * inv * q
        v_ref[s] = (inv * u).astype(BF)
        w_ref[s] = (-kap * r).astype(BF)
        kmat = jnp.where(lane == s, k, kmat)
        kap = kap + k

    unit = (
        lax.broadcasted_iota(jnp.int32, (CALLS, rank), 0) == lax.broadcasted_iota(jnp.int32, (CALLS, rank), 1)
    ).astype(F32)
    krows = lax.dot_general(unit, kmat, NT, precision=lax.Precision.HIGHEST, preferred_element_type=F32)

    quarter, eighth = cols // 4, cols // 8
    filler = jnp.zeros((out_ref.shape[1] - quarter - eighth, rank), F32)
    h_ref[0] = et_ref[...]
    for t in range(CALLS):
        h = h_ref[t]
        top = dot(h, v_ref[t]).astype(BF)
        low = dot(et_ref[...], v_ref[t]).astype(BF)
        for j in range(4):
            out_ref[t * 4 + j, :quarter] = top[j * quarter : (j + 1) * quarter]
            out_ref[CALLS * 4 + t * 4 + j, :quarter] = low[j * quarter : (j + 1) * quarter]
        if t + 1 < CALLS:
            h_ref[t + 1] = (h.astype(F32) + dot_nt(bt_ref[t], r_ref[t])).astype(BF)
    back = ct_ref[...]
    acc_ref[...] = jnp.zeros(acc_ref.shape, F32)
    for t in reversed(range(CALLS)):
        part = dot(back, r_ref[t])
        for j in range(8):
            piece = jnp.concatenate([part[j * eighth : (j + 1) * eighth], filler], axis=0)
            out_ref[t * 8 + j, quarter:] = piece.astype(BF)
        krow = krows[t : t + 1]
        step = dot_nt(a1_ref[t], v_ref[t]) - krow * h_ref[t].astype(F32)
        back = (back.astype(F32) + step).astype(BF)
        acc_ref[...] += dot_nt(a2_ref[t], v_ref[t]) - krow * et_ref[...].astype(F32)
    ge_ref[...] = (acc_ref[...] + back.astype(F32)).astype(BF)


def solve(proj, e2, gram, et, ct, a1, a2, bt):
    cols, tokens = et.shape
    rank = bt.shape[-1]
    vmem = pl.BlockSpec(memory_space=pltpu.VMEM)
    return pl.pallas_call(
        solve_kernel,
        out_shape=[
            jax.ShapeDtypeStruct((64, cols // 4 + 64, rank), BF),
            jax.ShapeDtypeStruct((cols, tokens), BF),
        ],
        in_specs=[vmem] * 8,
        out_specs=[vmem] * 2,
        scratch_shapes=[
            pltpu.VMEM((CALLS, tokens, rank), BF),
            pltpu.VMEM((CALLS, tokens, rank), BF),
            pltpu.VMEM((CALLS, tokens, rank), BF),
            pltpu.VMEM((CALLS, tokens, rank), F32),
            pltpu.VMEM((CALLS, cols, tokens), BF),
            pltpu.VMEM((cols, tokens), F32),
        ],
        compiler_params=pltpu.CompilerParams(vmem_limit_bytes=48 * 2**20),
    )(proj, e2, gram, et, ct, a1, a2, bt)


def per_device(embeds, cotangent, adapter_a, adapter_b, norm_gains):
    sec = lax.axis_index("section")
    dp = lax.axis_index("dp")
    width = embeds.shape[1]
    cols = width // CALLS
    a_own = adapter_a[0]
    quarter, rank = a_own.shape
    eighth = quarter // 2
    b_pad = jnp.pad(adapter_b[0].T, ((0, 64 - eighth), (0, 0)))
    gain = jnp.where(sec % 2 == 0, norm_gains[0], norm_gains[1])
    gain_rows = lax.dynamic_slice_in_dim(gain, dp * quarter, quarter, 0)
    gain_rows = jnp.broadcast_to(gain_rows[:, None], (quarter, rank))
    a_scaled = (a_own.astype(F32) * gain_rows).astype(BF)
    first, second = (jnp.pad(a_scaled[i : i + eighth], ((0, 64 - eighth), (0, 0))) for i in (0, eighth))
    upper = dp < 32
    sheet = gather_weights(
        a_scaled, b_pad, jnp.where(upper, first, second), jnp.where(upper, second, first), 0
    )
    sheet = sheet.reshape(64, 2 * quarter + 64, rank)
    pmat = sheet[:, :eighth].reshape(2, 32, eighth, rank).transpose(1, 0, 2, 3).reshape(width, rank)
    up = sheet[:, eighth:quarter].reshape(width, rank)
    parts = sheet[:, quarter : 2 * quarter].reshape(2, CALLS, cols, rank)
    bt_cols = sheet[:, 2 * quarter : 2 * quarter + eighth].reshape(CALLS, cols, rank)

    lead, spot = dp // 16, dp % 16
    early = spot < 15 - 2 * lead
    row = jnp.where(early, lead, CALLS - 1 - lead)
    pos = jnp.where(early, 2 * lead + spot, spot - 1)
    col = (pos + 1) // 2
    right = jnp.where(pos % 2 == 0, bt_cols[col], parts[0, col])
    gpart = lax.dot_general(bt_cols[row], right, (((0,), (0,)), ((), ())), preferred_element_type=F32)
    gpart = gpart.astype(BF).reshape(CALLS, 16, rank)
    proj = jnp.concatenate([dot(embeds, jnp.concatenate([pmat, up], axis=1)), dot(cotangent, up)], axis=1)
    gram, proj = gather_middle(gpart, proj.astype(BF), 1)
    gram = gram.reshape(64, rank, rank)
    proj = proj.reshape(CALLS, embeds.shape[0], 3 * rank)

    esq = embeds.astype(F32)
    e2 = jnp.broadcast_to(jnp.sum(esq * esq, axis=1, keepdims=True), (embeds.shape[0], rank))
    et = lax.dynamic_slice_in_dim(embeds, sec * cols, cols, 1).T
    ct = lax.dynamic_slice_in_dim(cotangent, sec * cols, cols, 1).T
    terms, ge = solve(proj, e2, gram, et, ct, parts[0], parts[1], bt_cols)

    grad_a, gb, gains = finish(terms, a_own, gain_rows, 2)
    grad_gain = jnp.sum(gains.reshape(CALLS // 2, 2, 8, rank)[:, :, 0, :quarter], axis=0)
    grad_b = gb.reshape(64, 64, rank)[:, :eighth].reshape(width, rank)
    return (grad_a[None], grad_b.T.astype(F32)[None], grad_gain, ge.T)


def solution(mesh):
    in_specs = (
        P("dp", None),
        P("dp", None),
        P("section", "dp", None),
        P("section", None, "dp"),
        P(),
    )
    out_specs = (
        P("section", "dp", None),
        P("section", None, None),
        P(None, "dp"),
        P("dp", "section"),
    )
    return jax.shard_map(per_device, mesh=mesh, in_specs=in_specs, out_specs=out_specs, check_vma=False)
```

time: 262 us -> 193 us (0.74)
  the two profiles are of different devices: /device:TPU:6 before, /device:TPU:57 now
where the time goes in v2:
time: 193 us; the launch traced here: 192 us
  Pallas kernels  167 us (87%)
  local copies, waits for them, and re-layouts  16.5 us (9%)
  other arithmetic  5.48 us (3%)
    pallas_call x1, Pallas kernels, finish(): pl.pallas_call(functools.partial(finish_kernel, dims, count), out_shape=[...  60.3 us
    pallas_call x1, Pallas kernels, gather_weights(): pl.pallas_call(functools.partial(weights_kernel, dims, count), out_shape=...  55.1 us
    pallas_call x1, Pallas kernels, gather_middle(): pl.pallas_call(functools.partial(middle_kernel, dims, secs), out_shape=[j...  40 us
    pallas_call x1, Pallas kernels, solve(): pl.pallas_call(solve_kernel, out_shape=[jax.ShapeDtypeStruct((64, cols //...  11.9 us
    unnamed x17, local copies, waits for them, and re-layouts  7.24 us

profile of v2, /device:TPU:57, one launch (start us, length us, event | category | flops | bytes accessed | tf_op | source)
XLA Modules:
  0.0 192.0 jit_solution(15370535732579967266)
XLA Ops:
  0.6 0.9 fusion.22
  1.7 0.8 multiply_convert_fusion.a_ref
  2.5 1.3 broadcast_select_fusion
  3.9 1.3 pad.10.b_ref
  5.2 55.1 %shard_map.84 = bf16[4,8,2,288,128]{4,3,2,1,0:T(8,128)(2,1)} custom-call(bf16[112,128]{1,0:T(8,128)(2,1)} %copy-done.5, bf16[64,128]{1,0:T(8,128)(2,1)} %pad.10.b_ref, bf16[64,128]{1,0:T(8,128)(2,1)} %get-tuple-element.34.keep_ref, bf16[64,128]{1,0:T(8,128)(2,1)} %get-tuple-element.33.give_ref), custom_call_target="tpu_custom_call" | custom-call | tf_op jit(solution)/shard_map/pallas_call | solution.py:207
  60.3 2.2 %fusion.21 = (bf16[64,56,128]{2,1,0:T(8,128)(2,1)S(1)}, bf16[64,56,128]{2,1,0:T(8,128)(2,1)S(1)}, bf16[64,56,128]{2,1,0:T(8,128)(2,1)S(1)}) fusion(bf16[64,288,128]{2,1,0:T(8,128)(2,1)} %bitcast.65), kind=kLoop, calls=%fused_computation.33 | loop fusion | bytes 5505024 | tf_op jit(solution)/shard_map/slice | solution.py:647
  62.6 1.2 copy-done.4
  63.9 0.5 fusion.7
  64.4 0.8 copy-done.3
  65.2 0.5 fusion.10
  65.8 0.7 pad_maximum_fusion.proj_ref
  66.4 1.6 slice.56
  68.1 0.8 convolution_convert_fusion.1
  68.9 40.0 %shard_map.85 = (bf16[4,8,2,8,16,128]{5,4,3,2,1,0:T(8,128)(2,1)}, bf16[2,4,192,384]{3,2,1,0:T(8,128)(2,1)}) custom-call(bf16[8,16,128]{2,1,0:T(8,128)(2,1)} %bitcast.74, bf16[192,384]{1,0:T(8,128)(2,1)} %pad_maximum_fusion.proj_ref), custom_call_target="tpu_custom_call" | custom-call | tf_op jit(solution)/shard_map/pallas_call | solution.py:300
  108.9 1.6 fusion.20
  110.5 1.2 constant_dynamic-slice_fusion
  112.1 1.8 multiply_reduce_fusion
  114.0 11.9 %shard_map.86 = (bf16[64,176,128]{2,1,0:T(8,128)(2,1)}, bf16[448,192]{1,0:T(8,128)(2,1)S(1)}) custom-call(bf16[8,192,384]{2,1,0:T(8,128)(2,1)S(1)} %bitcast.57, f32[192,128]{1,0:T(8,128)S(1)} %broadcast_in_dim.22.e2_ref, bf16[64,128,128]{2,1,0:T(8,128)(2,1)} %bitcast.71, bf16[448,192]{1,0:T(8,128)(2,1)S(1)} %bitcast.58, bf16[448,192]{1,0:T(8,128)(2,1)S(1)} %bitcast.59, ...), custom_call_target="tpu_custom_call" | custom-call | tf_op jit(solution)/shard_map/pallas_call | solution.py:608
  126.0 1.8 copy-done
  127.8 60.3 %shard_map.87 = (f32[112,128]{1,0:T(8,128)S(1)}, bf16[4,8,2,64,128]{4,3,2,1,0:T(8,128)(2,1)S(1)}, f32[8,8,128]{2,1,0:T(8,128)S(1)}) custom-call(bf16[4,8,2,176,128]{4,3,2,1,0:T(8,128)(2,1)S(1)} %bitcast.56, bf16[112,128]{1,0:T(8,128)(2,1)S(1)} %bitcast.62, f32[112,128]{1,0:T(8,128)S(1)} %broadcast_in_dim.21.gain_ref), custom_call_target="tpu_custom_call" | custom-call | tf_op jit(solution)/shard_map/pallas_call | solution.py:471
  188.3 1.7 copy.17
  190.0 0.6 slice_reduce_fusion
  190.6 0.8 copy.18
  191.4 0.6 copy.22
  (18 shorter events, 0.9 us)
Async XLA Ops:
  2.5 2.7 %copy-start.5 = (bf16[112,128]{1,0:T(8,128)(2,1)}, bf16[112,128]{1,0:T(8,128)(2,1)S(1)}, u32[]{:S(2)}) copy-start(bf16[112,128]{1,0:T(8,128)(2,1)S(1)} %multiply_convert_fusion.a_ref) | copy-start | bytes 86020
  62.5 1.3 copy-start.4
  63.9 1.3 copy-start.3
  112.1 1.9 copy-start.1
  114.0 12.0 %copy-start.2 = (bf16[1,112,128]{2,1,0:T(8,128)(2,1)S(1)}, bf16[1,112,128]{2,1,0:T(8,128)(2,1)}, u32[]{:S(2)}) copy-start(bf16[1,112,128]{2,1,0:T(8,128)(2,1)} %param.7) | copy-start | bytes 86020
  126.0 1.8 copy-start

commit v3 on v0

v3 whole, which is shorter than its diff:
```python
import functools

import jax
import jax.numpy as jnp
from jax import lax
from jax.experimental import pallas as pl
from jax.experimental.pallas import tpu as pltpu
from jax.sharding import PartitionSpec as P

EPS = 1e-05
CALLS = 8
DP = (4, 8, 2)
SEC = (2, 4)
BF = jnp.bfloat16
F32 = jnp.float32
MESH = pl.DeviceIdType.MESH
NT = (((1,), (1,)), ((), ()))


class Entry:
    def __init__(self, peers, swaps=()):
        self.sem = pltpu.get_barrier_semaphore()
        self.count = len(peers)
        for peer in peers:
            pl.semaphore_signal(self.sem, inc=1, device_id=peer, device_id_type=MESH)
        for swap in swaps:
            swap.greet(self.sem)
            self.count = self.count + jnp.where(swap.stays, 0, 1)

    def wait(self):
        pl.semaphore_wait(self.sem, self.count)


def remote(src, dst, send, recv, peer):
    return pltpu.make_async_remote_copy(
        src_ref=src, dst_ref=dst, send_sem=send, recv_sem=recv, device_id=peer, device_id_type=MESH
    )


def hops(zs, stream, ys):
    long_way, short_way = zs // 2, zs - 1 - zs // 2
    return (long_way, short_way) if stream < ys // 2 else (short_way, long_way)


class Ring:
    def __init__(self, dims):
        self.dims = dims
        ys, zs, cs = dims
        me = lax.axis_index("dp")
        self.y, self.z, self.c = me // (zs * cs), lax.rem(me // cs, zs), lax.rem(me, cs)
        self.rows = [self.at(lax.rem(self.y + j, ys), self.z, self.c) for j in range(1, ys)]
        right, left = lax.rem(self.z + 1, zs), lax.rem(self.z + zs - 1, zs)
        self.sides = (self.at(self.y, right, self.c), self.at(self.y, left, self.c))
        self.sibling = self.at(self.y, self.z, 1 - self.c)
        self.peers = self.rows + list(self.sides) + [self.sibling]

    def at(self, y, z, c):
        _, zs, cs = self.dims
        return {"dp": (y * zs + z) * cs + c}


def ring_sems(dims):
    ys, zs, _ = dims
    dma = pltpu.SemaphoreType.DMA
    return [
        dma,
        dma((ys,)),
        dma((ys,)),
        dma((2, ys, zs // 2)),
        dma((2, ys, zs // 2)),
        dma((ys, zs)),
        dma((ys, zs)),
    ]


class Spread:
    def __init__(self, ring, src, out_ref, sems):
        self.ring, self.src, self.out, self.sems = ring, src, out_ref, sems
        self.sent = []
        ys = ring.dims[0]
        self.lines = [lax.rem(ring.y + ys - j, ys) for j in range(ys)]

    def push(self, *what):
        copy = remote(*what)
        copy.start()
        self.sent.append(copy)

    def origin(self, side, k):
        zs = self.ring.dims[1]
        return lax.rem(self.ring.z + (zs - k if side == 0 else k), zs)

    def start(self):
        ring = self.ring
        local_sem, ysend, yrecv = self.sems[:3]
        block = self.out.at[ring.y, ring.z, ring.c]
        self.own = pltpu.make_async_copy(self.src, block, local_sem)
        self.own.start()
        for j in range(1, ring.dims[0]):
            self.push(self.src, block, ysend.at[j], yrecv.at[j], ring.rows[j - 1])

    def relay(self, j, side, k):
        ring = self.ring
        zsend, zrecv = self.sems[3:5]
        block = self.out.at[self.lines[j], self.origin(side, k), ring.c]
        src = block if j or k else self.src
        self.push(src, block, zsend.at[side, j, k], zrecv.at[side, j, k], ring.sides[side])

    def share(self, j, z, index):
        ring = self.ring
        csend, crecv = self.sems[5:7]
        block = self.out.at[self.lines[j], z, ring.c]
        src = block if j or index else self.src
        self.push(src, block, csend.at[j, index], crecv.at[j, index], ring.sibling)

    def first(self):
        ring = self.ring
        ys, zs, _ = ring.dims
        ysend, yrecv = self.sems[1:3]
        for j in range(ys):
            if j:
                block = self.out.at[self.lines[j], ring.z, ring.c]
                remote(block, block, ysend.at[j], yrecv.at[j], ring.rows[j - 1]).wait_recv()
            for side in range(2):
                if hops(zs, j, ys)[side]:
                    self.relay(j, side, 0)
            self.share(j, ring.z, 0)

    def step(self, k):
        ring = self.ring
        ys, zs, _ = ring.dims
        zsend, zrecv = self.sems[3:5]
        for j in range(ys):
            for side in range(2):
                count = hops(zs, j, ys)[side]
                if k <= count:
                    z = self.origin(side, k)
                    block = self.out.at[self.lines[j], z, ring.c]
                    remote(
                        block, block, zsend.at[side, j, k - 1], zrecv.at[side, j, k - 1], ring.sides[side]
                    ).wait_recv()
                    if k < count:
                        self.relay(j, side, k)
                    self.share(j, z, zs - k if side == 0 else k)

    def finish(self):
        ring = self.ring
        ys, zs, _ = ring.dims
        csend, crecv = self.sems[5:7]
        for j in range(ys):
            for index in range(zs):
                block = self.out.at[self.lines[j], lax.rem(ring.z + index, zs), 1 - ring.c]
                remote(block, block, csend.at[j, index], crecv.at[j, index], ring.sibling).wait_recv()
        self.own.wait()
        for copy in self.sent:
            copy.wait_send()

    def run(self, between=None):
        self.start()
        self.first()
        if between is not None:
            between()
        for k in range(1, self.ring.dims[1] // 2 + 1):
            self.step(k)
        self.finish()


class Swap:
    def __init__(self, section, dp):
        self.peer = {"section": section, "dp": dp}
        self.stays = section == lax.axis_index("section")

    def greet(self, sem):
        @pl.when(jnp.logical_not(self.stays))
        def _():
            pl.semaphore_signal(sem, inc=1, device_id=self.peer, device_id_type=MESH)

    def start(self, src, dst, sems):
        self.local = pltpu.make_async_copy(src, dst, sems.at[0])
        self.remote = remote(src, dst, sems.at[1], sems.at[2], self.peer)

        @pl.when(self.stays)
        def _():
            self.local.start()

        @pl.when(jnp.logical_not(self.stays))
        def _():
            self.remote.start()

    def wait(self):
        @pl.when(self.stays)
        def _():
            self.local.wait()

        @pl.when(jnp.logical_not(self.stays))
        def _():
            self.remote.wait()


def swap_down(dims, count):
    size = dims[0] * dims[1] * dims[2]
    half, step = size // 2, size // 2 // count
    sec, dp = lax.axis_index("section"), lax.axis_index("dp")
    return Swap(lax.rem(dp, half) // step, dp // half * half + sec * step + lax.rem(dp, step))


def swap_up(dims, count):
    step = dims[0] * dims[1] * dims[2] // count
    sec, dp = lax.axis_index("section"), lax.axis_index("dp")
    return Swap(dp // step, sec * step + lax.rem(dp, step))


def dot(a, b):
    return jnp.dot(a, b, preferred_element_type=F32)


def dot_nt(a, b):
    return lax.dot_general(a, b, NT, preferred_element_type=F32)


def eye(rows, cols, shift=0, kind=BF):
    row = lax.broadcasted_iota(jnp.int32, (rows, cols), 0)
    col = lax.broadcasted_iota(jnp.int32, (rows, cols), 1)
    return (col == row + shift).astype(F32).astype(kind)


def weights_kernel(
    dims,
    count,
    a_ref,
    b_ref,
    gain_ref,
    sec_ref,
    col_ref,
    scaled,
    b_rows,
    give,
    other,
    own_sec,
    own_col,
    hsend,
    hrecv,
    asems,
    bsems,
    *sems,
):
    ring = Ring(dims)
    down, up = swap_down(dims, count), swap_up(dims, count)
    entry = Entry(ring.peers, (down, up))
    rows, rank = a_ref.shape
    high = b_rows.shape[0]
    half = rows // 2
    value = (a_ref[...].astype(F32) * gain_ref[...]).astype(BF)
    scaled[...] = value
    turned = lax.dot_general(eye(high, half), b_ref[...], NT, preferred_element_type=F32)
    b_rows[...] = turned.astype(BF)
    value = value.astype(F32)
    upper = ring.y < dims[0] // 2
    rest = jnp.where(upper, value[half:], value[:half])
    if high > half:
        rest = jnp.concatenate([rest, jnp.zeros((high - half, rank), F32)], axis=0)
    give[...] = rest.astype(BF)
    entry.wait()
    exchange = remote(give, other, hsend, hrecv, ring.rows[dims[0] // 2 - 1])
    exchange.start()
    down.start(scaled, own_col.at[pl.ds(0, rows)], asems)
    up.start(b_rows, own_col.at[pl.ds(rows, high)], bsems)
    exchange.wait_recv()
    both = jnp.where(upper, value[:half], value[half:]) + other[...].astype(F32)[:half]
    own_sec[...] = jnp.concatenate([both, turned[:half]], axis=0).astype(BF)
    first = Spread(ring, own_sec, sec_ref, sems[: len(sems) // 2])
    second = Spread(ring, own_col, col_ref, sems[len(sems) // 2 :])
    first.start()
    first.first()
    last = dims[1] // 2
    first.step(1)
    down.wait()
    up.wait()
    second.start()
    for k in range(2, last + 1):
        first.step(k)
        if k == 2:
            second.first()
        else:
            second.step(k - 2)
    if last < 2:
        second.first()
    for k in range(max(1, last - 1), last + 1):
        second.step(k)
    first.finish()
    second.finish()
    exchange.wait_send()


def gather_weights(a, b, gain, collective_id, dims=DP, count=CALLS, high=64):
    rows, rank = a.shape
    dma = pltpu.SemaphoreType.DMA
    vmem = pl.BlockSpec(memory_space=pltpu.VMEM)
    anywhere = pl.BlockSpec(memory_space=pl.ANY)
    tall = rows + high
    return pl.pallas_call(
        functools.partial(weights_kernel, dims, count),
        out_shape=[
            jax.ShapeDtypeStruct(dims + (rows, rank), BF),
            jax.ShapeDtypeStruct(dims + (tall, rank), BF),
        ],
        in_specs=[vmem] * 3,
        out_specs=[anywhere] * 2,
        scratch_shapes=[pltpu.VMEM((n, rank), BF) for n in (rows, high, high, high, rows, tall)]
        + [dma, dma, dma((3,)), dma((3,))]
        + ring_sems(dims) * 2,
        compiler_params=pltpu.CompilerParams(
            collective_id=collective_id, has_side_effects=True, vmem_limit_bytes=16 * 2**20
        ),
    )(a, b, gain)


def middle_kernel(
    dims,
    secs,
    gram_ref,
    proj_ref,
    e_ref,
    c_ref,
    gall_ref,
    pall_ref,
    et_ref,
    ct_ref,
    e2_ref,
    landing,
    total_ref,
    send1,
    recv1,
    send2,
    recv2,
    local_sem,
    across_send,
    across_recv,
    xsend,
    xrecv,
    *sems,
):
    ring = Ring(dims)
    count, width = secs[0] * secs[1], secs[1]
    me = lax.axis_index("section")
    y0, x0 = me // width, lax.rem(me, width)
    peers = [{"section": lax.rem(me + j, count)} for j in range(1, count)]
    across = {"section": (1 - y0) * width + x0}
    beside = [{"section": y0 * width + lax.rem(x0 + j, width)} for j in range(1, width)]
    entry = Entry(ring.peers + peers)
    entry.wait()
    sent = []

    def push(*what):
        copy = remote(*what)
        copy.start()
        sent.append(copy)

    for j in range(1, count):
        push(gram_ref.at[lax.rem(me + j, count)], landing.at[me], send1.at[j], recv1.at[j], peers[j - 1])
    cols, tokens = et_ref.shape
    odd = 64 if cols % 128 else 0
    begin = me * cols
    shift = begin - begin // 128 * 128
    window = pl.ds(pl.multiple_of(begin // 128 * 128, 128), cols + odd)
    pick = eye(cols, cols + odd, shift)
    et_ref[...] = dot_nt(pick, e_ref[:, window]).astype(BF)
    ct_ref[...] = dot_nt(pick, c_ref[:, window]).astype(BF)
    square = jnp.zeros((tokens, 128), F32)
    for i in range(e_ref.shape[1] // 128):
        piece = e_ref[:, i * 128 : (i + 1) * 128].astype(F32)
        square = square + piece * piece
    e2_ref[...] = jnp.broadcast_to(jnp.sum(square, axis=1, keepdims=True), (tokens, 128))
    total = gram_ref[me].astype(F32)
    for j in range(1, count):
        source = lax.rem(me + count - j, count)
        block = landing.at[source]
        remote(block, block, send1.at[j], recv1.at[j], peers[j - 1]).wait_recv()
        total = total + landing[source].astype(F32)
    total_ref[me] = total.astype(total_ref.dtype)
    for j in range(1, count):
        push(total_ref.at[me], total_ref.at[me], send2.at[j], recv2.at[j], peers[j - 1])
    own = pltpu.make_async_copy(proj_ref, pall_ref.at[y0, x0], local_sem)
    own.start()
    push(proj_ref, pall_ref.at[y0, x0], across_send, across_recv, across)
    for j in range(1, width):
        push(proj_ref, pall_ref.at[y0, x0], xsend.at[0, j], xrecv.at[0, j], beside[j - 1])
    for j in range(1, count):
        block = total_ref.at[lax.rem(me + count - j, count)]
        remote(block, block, send2.at[j], recv2.at[j], peers[j - 1]).wait_recv()

    def forward():
        block = pall_ref.at[1 - y0, x0]
        remote(block, block, across_send, across_recv, across).wait_recv()
        for j in range(1, width):
            push(block, block, xsend.at[1, j], xrecv.at[1, j], beside[j - 1])

    Spread(ring, total_ref, gall_ref, sems).run(forward)
    for h in range(2):
        for j in range(1, width):
            landed = pall_ref.at[y0 if h == 0 else 1 - y0, lax.rem(x0 + width - j, width)]
            remote(landed, landed, xsend.at[h, j], xrecv.at[h, j], beside[j - 1]).wait_recv()
    own.wait()
    for copy in sent:
        copy.wait_send()


def gather_middle(gram, proj, embeds, cotangent, collective_id, dims=DP, secs=SEC):
    dma = pltpu.SemaphoreType.DMA
    count = secs[0] * secs[1]
    tokens, width = embeds.shape
    vmem = pl.BlockSpec(memory_space=pltpu.VMEM)
    anywhere = pl.BlockSpec(memory_space=pl.ANY)
    return pl.pallas_call(
        functools.partial(middle_kernel, dims, secs),
        out_shape=[
            jax.ShapeDtypeStruct(dims + gram.shape, gram.dtype),
            jax.ShapeDtypeStruct(secs + proj.shape, proj.dtype),
            jax.ShapeDtypeStruct((width // count, tokens), BF),
            jax.ShapeDtypeStruct((width // count, tokens), BF),
            jax.ShapeDtypeStruct((tokens, 128), F32),
        ],
        in_specs=[vmem, anywhere, vmem, vmem],
        out_specs=[anywhere, anywhere, vmem, vmem, vmem],
        scratch_shapes=[pltpu.VMEM(gram.shape, gram.dtype)] * 2
        + [dma((count,))] * 4
        + [dma, dma, dma, dma((2, secs[1])), dma((2, secs[1]))]
        + ring_sems(dims),
        compiler_params=pltpu.CompilerParams(
            collective_id=collective_id, has_side_effects=True, vmem_limit_bytes=32 * 2**20
        ),
    )(gram, proj, embeds, cotangent)


class Scatter:
    def __init__(self, ring, x_ref, rows, buffers, sems):
        self.ring, self.x, self.rows = ring, x_ref, rows
        self.from_core, self.moving, self.landing, self.rest, self.from_row = buffers
        self.sems = sems
        self.sent = []
        self.ready = set()
        self.totals = {}

    def push(self, *what):
        copy = remote(*what)
        copy.start()
        self.sent.append(copy)

    def start(self):
        ring = self.ring
        zs = ring.dims[1]
        csend, crecv = self.sems[:2]
        for offset in sorted(range(zs), key=lambda o: -min(o, zs - o)):
            z = lax.rem(ring.z + offset, zs)
            self.push(
                self.x.at[:, z, 1 - ring.c, self.rows],
                self.from_core.at[offset],
                csend.at[offset],
                crecv.at[offset],
                ring.sibling,
            )

    def need(self, offset):
        csend, crecv = self.sems[:2]
        if offset not in self.ready:
            self.ready.add(offset)
            block = self.from_core.at[offset]
            remote(block, block, csend.at[offset], crecv.at[offset], self.ring.sibling).wait_recv()

    def local_sum(self, offset, j):
        self.need(offset)
        ring = self.ring
        z = lax.rem(ring.z + offset, ring.dims[1])
        return self.x[j, z, ring.c, self.rows].astype(F32) + self.from_core[offset, j].astype(F32)

    def step(self, k):
        ring = self.ring
        ys, zs, _ = ring.dims
        zsend, zrecv = self.sems[2:4]
        for j in range(ys):
            for side in range(2):
                count = hops(zs, j, ys)[side]
                step = k - (zs // 2 - count)
                if step < 0:
                    continue
                reach = count - step
                offset = reach if side == 0 else (zs - reach) % zs
                got = 0.0
                if step:
                    spot = (side, j, step - 1)
                    block = self.landing.at[spot]
                    remote(block, block, zsend.at[spot], zrecv.at[spot], ring.sides[side]).wait_recv()
                    got = self.landing[spot].astype(F32)
                if reach:
                    spot = (side, j, step)
                    self.moving[spot] = (self.local_sum(offset, j) + got).astype(BF)
                    self.push(
                        self.moving.at[spot], self.landing.at[spot], zsend.at[spot], zrecv.at[spot], ring.sides[side]
                    )
                elif j not in self.totals:
                    self.totals[j] = self.local_sum(0, j) + got
                else:
                    self.rest[j] = (self.totals[j] + got).astype(BF)

    def rows_start(self):
        ring = self.ring
        ys = ring.dims[0]
        ysend, yrecv = self.sems[4:6]
        for i in range(1, ys):
            row = lax.rem(ring.y + i, ys)
            self.push(self.rest.at[row], self.from_row.at[i], ysend.at[i], yrecv.at[i], ring.rows[i - 1])

    def rows_finish(self):
        ring = self.ring
        ysend, yrecv = self.sems[4:6]
        own = self.rest[ring.y].astype(F32)
        for i in range(1, ring.dims[0]):
            block = self.from_row.at[i]
            remote(block, block, ysend.at[i], yrecv.at[i], ring.rows[i - 1]).wait_recv()
            own = own + self.from_row[i].astype(F32)
        return own

    def finish(self):
        for copy in self.sent:
            copy.wait_send()


def scatter_buffers(dims, rows, rank):
    ys, zs, _ = dims
    block = (rows, rank)
    shapes = [(zs, ys), (2, ys, zs // 2), (2, ys, zs // 2), (ys,), (ys,)]
    return [pltpu.VMEM(shape + block, BF) for shape in shapes]


def scatter_sems(dims):
    ys, zs, _ = dims
    dma = pltpu.SemaphoreType.DMA
    return [dma((zs,)), dma((zs,)), dma((2, ys, zs // 2)), dma((2, ys, zs // 2)), dma((ys,)), dma((ys,))]


def finish_kernel(dims, count, compute, inputs, *refs):
    given, refs = refs[:inputs], refs[inputs:]
    a_ref, gain_ref, ga_ref, gb_ref, gg_ref, ge_ref, x_ref, mine_low, got_low, mine_high, got_high = refs[:11]
    low_buffers, high_buffers = refs[11:16], refs[16:21]
    low_sems, high_sems = refs[21:27], refs[27:33]
    asems, bsems, gsend, grecv = refs[33:37]
    ring_part = refs[37:44]
    scratch = refs[44:]
    ring = Ring(dims)
    down, up = swap_down(dims, count), swap_up(dims, count)
    me = lax.axis_index("section")
    peers = [{"section": lax.rem(me + j, count)} for j in range(1, count)]
    entry = Entry(ring.peers + peers, (down, up))
    rows, rank = a_ref.shape
    high = got_high.shape[0]
    upper = Scatter(ring, x_ref, pl.ds(rows, high), high_buffers, high_sems)
    lower = Scatter(ring, x_ref, pl.ds(0, rows), low_buffers, low_sems)
    work = compute(given, x_ref, ge_ref, scratch)
    work.ups()
    entry.wait()
    upper.start()
    upper.step(0)
    work.downs()
    lower.start()
    last = dims[1] // 2
    for k in range(1, last + 1):
        upper.step(k)
        if k > 1 or last == 1:
            lower.step(max(k - 2, 0))
    upper.rows_start()
    if last > 1:
        lower.step(last - 1)
    mine_high[...] = upper.rows_finish().astype(BF)
    up.start(mine_high, got_high, bsems)
    lower.step(last)
    lower.rows_start()
    work.rest()
    mine_low[...] = lower.rows_finish().astype(BF)
    down.start(mine_low, got_low, asems)
    up.wait()
    gather = Spread(ring, got_high, gb_ref, ring_part)
    gather.start()
    gather.first()
    down.wait()
    w = got_low[...].astype(F32)
    ga_ref[...] = w * gain_ref[...]
    prod = w * a_ref[...].astype(F32)
    if rank > rows:
        prod = jnp.concatenate([prod, jnp.zeros((rank - rows, rank), F32)], axis=0)
    line = lax.dot_general(
        jnp.ones((8, rank), F32), prod, NT, precision=lax.Precision.HIGHEST, preferred_element_type=F32
    )
    gg_ref[me] = line.astype(BF).astype(F32)
    sent = []
    for j in range(1, count):
        copy = remote(gg_ref.at[me], gg_ref.at[me], gsend.at[j], grecv.at[j], peers[j - 1])
        copy.start()
        sent.append(copy)
    for k in range(1, last + 1):
        gather.step(k)
    gather.finish()
    for j in range(1, count):
        block = gg_ref.at[lax.rem(me + count - j, count)]
        remote(block, block, gsend.at[j], grecv.at[j], peers[j - 1]).wait_recv()
    for copy in sent:
        copy.wait_send()
    upper.finish()
    lower.finish()


def finish(given, a, gain, ge_shape, compute, scratch, collective_id, dims=DP, count=CALLS, high=64):
    rows, rank = a.shape
    dma = pltpu.SemaphoreType.DMA
    vmem = pl.BlockSpec(memory_space=pltpu.VMEM)
    return pl.pallas_call(
        functools.partial(finish_kernel, dims, count, compute, len(given)),
        out_shape=[
            jax.ShapeDtypeStruct(a.shape, F32),
            jax.ShapeDtypeStruct(dims + (high, rank), BF),
            jax.ShapeDtypeStruct((count, 8, rank), F32),
            jax.ShapeDtypeStruct(ge_shape, BF),
        ],
        in_specs=[vmem] * (len(given) + 2),
        out_specs=[vmem, pl.BlockSpec(memory_space=pl.ANY), vmem, vmem],
        scratch_shapes=[pltpu.VMEM(dims + (rows + high, rank), BF)]
        + [pltpu.VMEM((n, rank), BF) for n in (rows, rows, high, high)]
        + scatter_buffers(dims, rows, rank)
        + scatter_buffers(dims, high, rank)
        + scatter_sems(dims) * 2
        + [dma((3,)), dma((3,)), dma((count,)), dma((count,))]
        + ring_sems(dims)
        + scratch,
        compiler_params=pltpu.CompilerParams(
            collective_id=collective_id, has_side_effects=True, vmem_limit_bytes=48 * 2**20
        ),
    )(*given, a, gain)


class Solver:
    def __init__(self, given, x_ref, ge_ref, scratch):
        self.given, self.x, self.ge = given, x_ref, ge_ref
        self.r, self.v, self.w, self.hb, self.h, self.acc = scratch
        self.col = given[5]

    def down_rows(self, half, t):
        quarter = self.h.shape[1] // 4
        first = half * 4 * CALLS + t * 4
        return jnp.concatenate([self.col[first + j, :quarter] for j in range(4)], axis=0)

    def up_rows(self, t):
        quarter = self.h.shape[1] // 4
        eighth = quarter // 2
        pieces = [self.col[t * 8 + j, quarter:].astype(F32)[:eighth] for j in range(8)]
        return jnp.concatenate(pieces, axis=0).astype(BF)

    def put(self, index, rows, value):
        self.x[index // 16, index // 2 % 8, index % 2, rows] = value

    def ups(self):
        proj_ref, e2_ref, gram_ref, et_ref, ct_ref, _ = self.given
        r_ref, v_ref, w_ref, hb_ref, h_ref, acc_ref = self.r, self.v, self.w, self.hb, self.h, self.acc
        tokens, rank = r_ref.shape[1:]
        cols = et_ref.shape[0]
        scale = 1.0 / (2 * cols * CALLS)

        def gram(t, pos):
            return gram_ref[14 * t + pos if 2 * t < CALLS else 16 * (CALLS - 1 - t) + pos + 1]

        e2 = e2_ref[:, :1]
        h2 = e2
        invs = []
        for s in range(CALLS):
            pre = proj_ref[s, :, :rank].astype(F32)
            hb = proj_ref[s, :, rank : 2 * rank].astype(F32)
            for t in range(s):
                pre = pre + dot(r_ref[t], gram(t, 2 * s - 1))
                hb = hb + dot(r_ref[t], gram(t, 2 * s))
            inv = lax.rsqrt((e2 + h2) * scale + EPS)
            invs.append(inv)
            r = (pre * inv).astype(BF)
            r_ref[s] = r
            rn = dot(r, gram(s, 2 * s))
            h2 = h2 + jnp.sum(r.astype(F32) * (2.0 * hb + rn), axis=1, keepdims=True)
            hb_ref[s] = hb + rn

        lane = lax.broadcasted_iota(jnp.int32, (tokens, rank), 1)
        kap = jnp.zeros((tokens, 1), F32)
        kmat = jnp.zeros((tokens, rank), F32)
        for s in reversed(range(CALLS)):
            u = proj_ref[s, :, 2 * rank :].astype(F32) - kap * hb_ref[s]
            for t in range(s + 1, CALLS):
                u = u + dot_nt(v_ref[t], gram(s, 2 * t - 1)) + dot_nt(w_ref[t], gram(s, 2 * t))
            u = u.astype(BF).astype(F32)
            r = r_ref[s].astype(F32)
            inv = invs[s]
            q = jnp.sum(u * r, axis=1, keepdims=True) * scale
            k = inv * inv * q
            v_ref[s] = (inv * u).astype(BF)
            w_ref[s] = (-kap * r).astype(BF)
            kmat = jnp.where(lane == s, k, kmat)
            kap = kap + k

        unit = (
            lax.broadcasted_iota(jnp.int32, (CALLS, rank), 0) == lax.broadcasted_iota(jnp.int32, (CALLS, rank), 1)
        ).astype(F32)
        krows = lax.dot_general(unit, kmat, NT, precision=lax.Precision.HIGHEST, preferred_element_type=F32)

        quarter, eighth = cols // 4, cols // 8
        filler = jnp.zeros((64 - eighth, rank), F32)
        h_ref[0] = et_ref[...]
        for t in range(CALLS - 1):
            h_ref[t + 1] = (h_ref[t].astype(F32) + dot_nt(self.up_rows(t), r_ref[t])).astype(BF)
        back = ct_ref[...]
        for t in reversed(range(CALLS)):
            part = dot(back, r_ref[t])
            for j in range(8):
                piece = jnp.concatenate([part[j * eighth : (j + 1) * eighth], filler], axis=0)
                self.put(t * 8 + j, pl.ds(quarter, 64), piece.astype(BF))
            step = dot_nt(self.down_rows(0, t), v_ref[t]) - krows[t : t + 1] * h_ref[t].astype(F32)
            back = (back.astype(F32) + step).astype(BF)
        total = back.astype(F32) - jnp.sum(krows, axis=0, keepdims=True) * et_ref[...].astype(F32)
        acc_ref[...] = total

    def downs(self):
        et_ref = self.given[3]
        quarter = self.h.shape[1] // 4
        for t in range(CALLS):
            for half, source in ((0, self.h[t]), (1, et_ref[...])):
                value = dot(source, self.v[t]).astype(BF)
                for j in range(4):
                    index = half * 4 * CALLS + t * 4 + j
                    self.put(index, pl.ds(0, quarter), value[j * quarter : (j + 1) * quarter])

    def rest(self):
        for t in range(CALLS):
            self.acc[...] += dot_nt(self.down_rows(1, t), self.v[t])
        self.ge[...] = self.acc[...].astype(BF)


def per_device(embeds, cotangent, adapter_a, adapter_b, norm_gains):
    sec = lax.axis_index("section")
    dp = lax.axis_index("dp")
    tokens, width = embeds.shape
    cols = width // CALLS
    a_own = adapter_a[0]
    quarter, rank = a_own.shape
    eighth = quarter // 2
    gain = jnp.where(sec % 2 == 0, norm_gains[0], norm_gains[1])
    gain_rows = lax.dynamic_slice_in_dim(gain, dp * quarter, quarter, 0)
    gain_rows = jnp.broadcast_to(gain_rows[:, None], (quarter, rank))
    own, col = gather_weights(a_own, adapter_b[0], gain_rows, 0)
    own = own.reshape(64, quarter, rank)
    col = col.reshape(64, quarter + 64, rank)
    pmat = own[:, :eighth].reshape(2, 32, eighth, rank).transpose(1, 0, 2, 3).reshape(width, rank)
    up = own[:, eighth:].reshape(width, rank)
    proj = jnp.concatenate([dot(embeds, jnp.concatenate([pmat, up], axis=1)), dot(cotangent, up)], axis=1)

    lead, spot = dp // 16, dp % 16
    early = spot < 15 - 2 * lead
    row = jnp.where(early, lead, CALLS - 1 - lead)
    pos = jnp.where(early, 2 * lead + spot, spot - 1)
    other = (pos + 1) // 2
    bt_of = lambda t: lax.dynamic_slice_in_dim(col, t * 8, 8, 0)[:, quarter : quarter + eighth].reshape(cols, rank)
    a1 = lax.dynamic_slice_in_dim(col, other * 4, 4, 0)[:, :quarter].reshape(cols, rank)
    right = jnp.where(pos % 2 == 0, bt_of(other), a1)
    gpart = lax.dot_general(bt_of(row), right, (((0,), (0,)), ((), ())), preferred_element_type=F32)
    gpart = gpart.astype(BF).reshape(CALLS, 16, rank)
    gram, proj, et, ct, e2 = gather_middle(gpart, proj.astype(BF), embeds, cotangent, 1)
    gram = gram.reshape(64, rank, rank)
    proj = proj.reshape(CALLS, tokens, 3 * rank)

    scratch = [
        pltpu.VMEM((CALLS, tokens, rank), BF),
        pltpu.VMEM((CALLS, tokens, rank), BF),
        pltpu.VMEM((CALLS, tokens, rank), BF),
        pltpu.VMEM((CALLS, tokens, rank), F32),
        pltpu.VMEM((CALLS, cols, tokens), BF),
        pltpu.VMEM((cols, tokens), F32),
    ]
    grad_a, gb, gains, ge = finish(
        (proj, e2, gram, et, ct, col), a_own, gain_rows, (cols, tokens), Solver, scratch, 2
    )
    grad_gain = jnp.sum(gains.reshape(CALLS // 2, 2, 8, rank)[:, :, 0, :quarter], axis=0)
    grad_b = gb.reshape(64, 64, rank)[:, :eighth].reshape(width, rank)
    return (grad_a[None], grad_b.T.astype(F32)[None], grad_gain, ge.T)


def solution(mesh):
    in_specs = (
        P("dp", None),
        P("dp", None),
        P("section", "dp", None),
        P("section", None, "dp"),
        P(),
    )
    out_specs = (
        P("section", "dp", None),
        P("section", None, None),
        P(None, "dp"),
        P("dp", "section"),
    )
    return jax.shard_map(per_device, mesh=mesh, in_specs=in_specs, out_specs=out_specs, check_vma=False)
```

time: 1960 us -> 166 us (0.08)
  the two profiles are of different devices: /device:TPU:4 before, /device:TPU:11 now
where the time goes in v3:
time: 166 us; the launch traced here: 165 us
  Pallas kernels  153 us (92%)
  local copies, waits for them, and re-layouts  8.95 us (5%)
    pallas_call x1, Pallas kernels, finish(): pl.pallas_call(functools.partial(finish_kernel, dims, count, compute, len...  62.8 us
    pallas_call x1, Pallas kernels, gather_weights(): pl.pallas_call(functools.partial(weights_kernel, dims, count), out_shape=...  50.8 us
    pallas_call x1, Pallas kernels, gather_middle(): pl.pallas_call(functools.partial(middle_kernel, dims, secs), out_shape=[j...  39.8 us
    unnamed x14, local copies, waits for them, and re-layouts  7.61 us

profile of v3, /device:TPU:11, one launch (start us, length us, event | category | flops | bytes accessed | tf_op | source)
XLA Modules:
  0.0 165.4 jit_solution(9832197162365516996)
XLA Ops:
  0.7 0.8 copy.13
  1.5 1.0 fusion.18
  2.5 0.1 fusion.15
  2.6 0.1 broadcast_in_dim.15.gain_ref.refs_7_
  2.7 0.8 copy-done.3
  3.4 50.8 %shard_map.84 = (bf16[4,8,2,112,128]{4,3,2,1,0:T(8,128)(2,1)S(1)}, bf16[4,8,2,176,128]{4,3,2,1,0:T(8,128)(2,1)S(1)}) custom-call(bf16[112,128]{1,0:T(8,128)(2,1)S(1)} %bitcast.46, bf16[128,56]{1,0:T(8,128)(2,1)S(1)} %bitcast.45, f32[112,128]{1,0:T(8,128)S(1)} %broadcast_in_dim.15.gain_ref.refs_7_), custom_call_target="tpu_custom_call" | custom-call | tf_op jit(solution)/shard_map/pallas_call | solution.py:300
  54.2 0.1 fusion.17
  54.4 0.0 copy-start.2
  54.4 0.1 copy.14
  54.5 2.1 %copy-done.2 = bf16[192,3584]{1,0:T(8,128)(2,1)S(1)} copy-done((bf16[192,3584]{1,0:T(8,128)(2,1)S(1)}, bf16[192,3584]{1,0:T(8,128)(2,1)}, u32[]{:S(2)}) %copy-start.2) | copy-done | bytes 1376280
  56.6 0.5 fusion.7
  57.2 0.8 copy-done
  58.0 0.5 fusion.11
  58.5 0.0 copy-start.4
  58.5 0.0 copy-done.1
  58.6 0.2 fusion.10
  58.8 39.8 %shard_map.85 = (bf16[4,8,2,8,16,128]{5,4,3,2,1,0:T(8,128)(2,1)S(1)}, bf16[2,4,192,384]{3,2,1,0:T(8,128)(2,1)S(1)}, bf16[448,192]{1,0:T(8,128)(2,1)S(1)}, bf16[448,192]{1,0:T(8,128)(2,1)S(1)}, f32[192,128]{1,0:T(8,128)S(1)}) custom-call(bf16[8,16,128]{2,1,0:T(8,128)(2,1)S(1)} %bitcast.49, bf16[192,384]{1,0:T(8,128)(2,1)S(1)} %pad_maximum_fusion.proj_ref, ...), custom_call_target="tpu_custom_call" | custom-call | tf_op jit(solution)/shard_map/pallas_call | solution.py:413
  98.6 62.8 %shard_map.86 = (f32[112,128]{1,0:T(8,128)S(1)}, bf16[4,8,2,64,128]{4,3,2,1,0:T(8,128)(2,1)S(1)}, f32[8,8,128]{2,1,0:T(8,128)S(1)}, bf16[448,192]{1,0:T(8,128)(2,1)S(1)}) custom-call(bf16[8,192,384]{2,1,0:T(8,128)(2,1)S(1)} %bitcast.42, f32[192,128]{1,0:T(8,128)S(1)} %get-tuple-element.18.refs_1_, bf16[64,128,128]{2,1,0:T(8,128)(2,1)S(1)} %bitcast.40, ...), custom_call_target="tpu_custom_call" | custom-call | tf_op jit(solution)/shard_map/pallas_call | solution.py:614
  161.4 0.1 slice.38
  161.5 0.6 slice_reduce_fusion
  162.1 0.8 copy.16
  162.9 0.2 convert_bitcast_fusion
  163.0 1.7 %copy.15 = f32[1,128,3584]{2,1,0:T(8,128)} copy(f32[1,128,3584]{1,2,0:T(8,128)S(1)} %convert_bitcast_fusion) | data formatting | bytes 3670016
  164.7 0.6 copy.18
  (6 shorter events, 0.0 us)
Async XLA Ops:
  2.7 0.8 copy-start.3
  54.2 4.3 %copy-start.1 = (bf16[4,8,2,176,128]{4,3,2,1,0:T(8,128)(2,1)}, bf16[4,8,2,176,128]{4,3,2,1,0:T(8,128)(2,1)S(1)}, u32[]{:S(2)}) copy-start(bf16[4,8,2,176,128]{4,3,2,1,0:T(8,128)(2,1)S(1)} %get-tuple-element.15) | copy-start | bytes 8650756
  54.4 2.2 %copy-start.2 = (bf16[192,3584]{1,0:T(8,128)(2,1)S(1)}, bf16[192,3584]{1,0:T(8,128)(2,1)}, u32[]{:S(2)}) copy-start(bf16[192,3584]{1,0:T(8,128)(2,1)} %e_ref.1) | copy-start | bytes 4128772
  56.6 1.3 copy-start
  58.5 40.1 %copy-start.4 = (bf16[1,112,128]{2,1,0:T(8,128)(2,1)S(1)}, bf16[1,112,128]{2,1,0:T(8,128)(2,1)}, u32[]{:S(2)}) copy-start(bf16[1,112,128]{2,1,0:T(8,128)(2,1)} %param.7) | copy-start | bytes 86020

commit v4 on v3

--- a/solution.py
+++ b/solution.py
@@ -77,6 +77,7 @@
     def __init__(self, ring, src, out_ref, sems):
         self.ring, self.src, self.out, self.sems = ring, src, out_ref, sems
         self.sent = []
+        self.own = None
         ys = ring.dims[0]
         self.lines = [lax.rem(ring.y + ys - j, ys) for j in range(ys)]
 
@@ -98,18 +99,21 @@
         for j in range(1, ring.dims[0]):
             self.push(self.src, block, ysend.at[j], yrecv.at[j], ring.rows[j - 1])
 
+    def await_own(self):
+        pass
+
     def relay(self, j, side, k):
         ring = self.ring
         zsend, zrecv = self.sems[3:5]
         block = self.out.at[self.lines[j], self.origin(side, k), ring.c]
-        src = block if j or k else self.src
+        src = block if j or k or self.src is None else self.src
         self.push(src, block, zsend.at[side, j, k], zrecv.at[side, j, k], ring.sides[side])
 
     def share(self, j, z, index):
         ring = self.ring
         csend, crecv = self.sems[5:7]
         block = self.out.at[self.lines[j], z, ring.c]
-        src = block if j or index else self.src
+        src = block if j or index or self.src is None else self.src
         self.push(src, block, csend.at[j, index], crecv.at[j, index], ring.sibling)
 
     def first(self):
@@ -120,6 +124,8 @@
             if j:
                 block = self.out.at[self.lines[j], ring.z, ring.c]
                 remote(block, block, ysend.at[j], yrecv.at[j], ring.rows[j - 1]).wait_recv()
+            else:
+                self.await_own()
             for side in range(2):
                 if hops(zs, j, ys)[side]:
                     self.relay(j, side, 0)
@@ -142,7 +148,7 @@
                         self.relay(j, side, k)
                     self.share(j, z, zs - k if side == 0 else k)
 
-    def finish(self):
+    def landed(self):
         ring = self.ring
         ys, zs, _ = ring.dims
         csend, crecv = self.sems[5:7]
@@ -150,18 +156,78 @@
             for index in range(zs):
                 block = self.out.at[self.lines[j], lax.rem(ring.z + index, zs), 1 - ring.c]
                 remote(block, block, csend.at[j, index], crecv.at[j, index], ring.sibling).wait_recv()
-        self.own.wait()
+        if self.own is not None:
+            self.own.wait()
+
+    def drain(self):
         for copy in self.sent:
             copy.wait_send()
 
-    def run(self, between=None):
-        self.start()
-        self.first()
-        if between is not None:
-            between()
-        for k in range(1, self.ring.dims[1] // 2 + 1):
-            self.step(k)
-        self.finish()
+    def finish(self):
+        self.landed()
+        self.drain()
+
+
+class Fan(Spread):
+    def __init__(self, ring, count, out_ref, sems):
+        super().__init__(ring, None, out_ref, sems)
+        ys, zs, cs = ring.dims
+        step = ys * zs * cs // count
+        sec, dp = lax.axis_index("section"), lax.axis_index("dp")
+        self.call, slot = dp // step, sec * step + lax.rem(dp, step)
+        self.stays = self.call == sec
+        self.slot = (slot // (zs * cs), lax.rem(slot // cs, zs), lax.rem(slot, cs))
+        self.targets, self.sources = [], []
+        for i in range(ys):
+            y = lax.rem(self.slot[0] + i, ys)
+            self.targets.append({"section": self.call, **ring.at(y, *self.slot[1:])})
+            place = (self.lines[i] * zs + ring.z) * cs + ring.c
+            self.sources.append({"section": place // step, "dp": sec * step + lax.rem(place, step)})
+
+    def greet(self, sem):
+        for peer in self.sources[1:]:
+            pl.semaphore_signal(sem, inc=1, device_id=peer, device_id_type=MESH)
+
+        @pl.when(jnp.logical_not(self.stays))
+        def _():
+            pl.semaphore_signal(sem, inc=1, device_id=self.sources[0], device_id_type=MESH)
+
+    def start_from(self, src):
+        local_sem, ysend, yrecv = self.sems[:3]
+        spot = self.out.at[self.slot]
+        self.local = pltpu.make_async_copy(src, spot, local_sem)
+        self.cross = remote(src, spot, ysend.at[0], yrecv.at[0], self.targets[0])
+
+        @pl.when(self.stays)
+        def _():
+            self.local.start()
+
+        @pl.when(jnp.logical_not(self.stays))
+        def _():
+            self.cross.start()
+
+        for i in range(1, self.ring.dims[0]):
+            self.push(src, spot, ysend.at[i], yrecv.at[i], self.targets[i])
+
+    def await_own(self):
+        ring = self.ring
+        block = self.out.at[ring.y, ring.z, ring.c]
+        ysend, yrecv = self.sems[1:3]
+
+        @pl.when(self.stays)
+        def _():
+            self.local.wait()
+
+        @pl.when(jnp.logical_not(self.stays))
+        def _():
+            remote(block, block, ysend.at[0], yrecv.at[0], self.targets[0]).wait_recv()
+
+    def drain(self):
+        super().drain()
+
+        @pl.when(jnp.logical_not(self.stays))
+        def _():
+            self.cross.wait_send()
 
 
 class Swap:
@@ -223,29 +289,85 @@
     return (col == row + shift).astype(F32).astype(kind)
 
 
-def weights_kernel(
-    dims,
-    count,
-    a_ref,
-    b_ref,
-    gain_ref,
-    sec_ref,
-    col_ref,
-    scaled,
-    b_rows,
-    give,
-    other,
-    own_sec,
-    own_col,
-    hsend,
-    hrecv,
-    asems,
-    bsems,
-    *sems,
-):
+class Front:
+    def __init__(self, sec_ref, col_ref, e_ref, c_ref, wide_ref, et_ref, ct_ref, e2_ref):
+        self.sec, self.col, self.e, self.c, self.wide = sec_ref, col_ref, e_ref, c_ref, wide_ref
+        self.et, self.ct, self.e2 = et_ref, ct_ref, e2_ref
+
+    def tokens(self):
+        cols, tokens = self.et.shape
+        odd = 64 if cols % 128 else 0
+        begin = lax.axis_index("section") * cols
+        start = begin // 128 * 128
+        window = pl.ds(pl.multiple_of(start, 128), cols + odd)
+        pick = eye(cols, cols + odd, begin - start)
+        self.et[...] = dot_nt(pick, self.e[:, window]).astype(BF)
+        self.ct[...] = dot_nt(pick, self.c[:, window]).astype(BF)
+        square = jnp.zeros((tokens, 128), F32)
+        for i in range(self.e.shape[1] // 128):
+            piece = self.e[:, i * 128 : (i + 1) * 128].astype(F32)
+            square = square + piece * piece
+        self.e2[...] = jnp.broadcast_to(jnp.sum(square, axis=1, keepdims=True), (tokens, 128))
+
+    def project(self, out_ref):
+        rows, rank = self.sec.shape[3:]
+        half = rows // 2
+        for i in range(32):
+            y, z, c = i // 16, i // 2 % 8, i % 2
+            low, high = self.sec[y, z, c].astype(F32), self.sec[y + 2, z, c].astype(F32)
+            both = jnp.concatenate([low[:half], high[:half]], axis=0)
+            self.wide[i * rows : (i + 1) * rows, :rank] = both.astype(BF)
+            low, high = self.sec[i // 8, i % 8, 0].astype(F32), self.sec[i // 8, i % 8, 1].astype(F32)
+            both = jnp.concatenate([low[half:], high[half:]], axis=0)
+            self.wide[i * rows : (i + 1) * rows, rank:] = both.astype(BF)
+        out_ref[:, : 2 * rank] = dot(self.e[...], self.wide[...]).astype(BF)
+        out_ref[:, 2 * rank :] = dot(self.c[...], self.wide[:, rank:]).astype(BF)
+
+    def block(self, index):
+        return self.col[index // 16, lax.rem(index // 2, 8), lax.rem(index, 2)].astype(F32)
+
+    def gram(self, out_ref):
+        quarter = self.et.shape[0] // 4
+        eighth = quarter // 2
+        dp = lax.axis_index("dp")
+        lead, spot = dp // 16, lax.rem(dp, 16)
+        early = spot < 15 - 2 * lead
+        row = jnp.where(early, lead, CALLS - 1 - lead)
+        pos = jnp.where(early, 2 * lead + spot, spot - 1)
+        other = (pos + 1) // 2
+        even = lax.rem(pos, 2) == 0
+        left = jnp.concatenate([self.block(row * 8 + j)[quarter:][:eighth] for j in range(8)], axis=0)
+        ups = jnp.concatenate([self.block(other * 8 + j)[quarter:][:eighth] for j in range(8)], axis=0)
+        downs = jnp.concatenate([self.block(other * 4 + j)[:quarter] for j in range(4)], axis=0)
+        right = jnp.where(even, ups, downs)
+        value = lax.dot_general(
+            left.astype(BF), right.astype(BF), (((0,), (0,)), ((), ())), preferred_element_type=F32
+        )
+        out_ref[...] = value.astype(BF)
+
+
+def front_kernel(dims, secs, make, *refs):
+    a_ref, b_ref, gain_ref, e_hbm, c_hbm = refs[:5]
+    col_out, gall_ref, pall_ref, et_ref, ct_ref, e2_ref = refs[5:11]
+    scaled, b_rows, give, other, own_sec, own_col = refs[11:17]
+    sec_ref, col_ref, e_ref, c_ref, wide_ref, proj_ref, gram_ref, landing, total_ref = refs[17:26]
+    load_e, load_c, save_col, hsend, hrecv, asems, bsems = refs[26:33]
+    gsend, grecv, local_sem, across_send, across_recv, xsend, xrecv = refs[33:40]
+    first_sems, second_sems, third_sems = refs[40:47], refs[47:54], refs[54:61]
     ring = Ring(dims)
+    count, width = secs[0] * secs[1], secs[1]
+    me = lax.axis_index("section")
+    y0, x0 = me // width, lax.rem(me, width)
+    peers = [{"section": lax.rem(me + j, count)} for j in range(1, count)]
+    across = {"section": (1 - y0) * width + x0}
+    beside = [{"section": y0 * width + lax.rem(x0 + j, width)} for j in range(1, width)]
     down, up = swap_down(dims, count), swap_up(dims, count)
-    entry = Entry(ring.peers, (down, up))
+    entry = Entry(ring.peers + peers, (down, up))
+    loads = [pltpu.make_async_copy(e_hbm, e_ref, load_e), pltpu.make_async_copy(c_hbm, c_ref, load_c)]
+    for load in loads:
+        load.start()
+    work = make(sec_ref, col_ref, e_ref, c_ref, wide_ref, et_ref, ct_ref, e2_ref)
+
     rows, rank = a_ref.shape
     high = b_rows.shape[0]
     half = rows // 2
@@ -264,14 +386,18 @@
     exchange.start()
     down.start(scaled, own_col.at[pl.ds(0, rows)], asems)
     up.start(b_rows, own_col.at[pl.ds(rows, high)], bsems)
+    for load in loads:
+        load.wait()
+    work.tokens()
     exchange.wait_recv()
     both = jnp.where(upper, value[:half], value[half:]) + other[...].astype(F32)[:half]
     own_sec[...] = jnp.concatenate([both, turned[:half]], axis=0).astype(BF)
-    first = Spread(ring, own_sec, sec_ref, sems[: len(sems) // 2])
-    second = Spread(ring, own_col, col_ref, sems[len(sems) // 2 :])
+    first = Spread(ring, own_sec, sec_ref, first_sems)
+    second = Spread(ring, own_col, col_ref, second_sems)
+    third = Spread(ring, total_ref, gall_ref, third_sems)
+    last = dims[1] // 2
     first.start()
     first.first()
-    last = dims[1] // 2
     first.step(1)
     down.wait()
     up.wait()
@@ -284,70 +410,8 @@
             second.step(k - 2)
     if last < 2:
         second.first()
-    for k in range(max(1, last - 1), last + 1):
-        second.step(k)
-    first.finish()
-    second.finish()
-    exchange.wait_send()
-
-
-def gather_weights(a, b, gain, collective_id, dims=DP, count=CALLS, high=64):
-    rows, rank = a.shape
-    dma = pltpu.SemaphoreType.DMA
-    vmem = pl.BlockSpec(memory_space=pltpu.VMEM)
-    anywhere = pl.BlockSpec(memory_space=pl.ANY)
-    tall = rows + high
-    return pl.pallas_call(
-        functools.partial(weights_kernel, dims, count),
-        out_shape=[
-            jax.ShapeDtypeStruct(dims + (rows, rank), BF),
-            jax.ShapeDtypeStruct(dims + (tall, rank), BF),
-        ],
-        in_specs=[vmem] * 3,
-        out_specs=[anywhere] * 2,
-        scratch_shapes=[pltpu.VMEM((n, rank), BF) for n in (rows, high, high, high, rows, tall)]
-        + [dma, dma, dma((3,)), dma((3,))]
-        + ring_sems(dims) * 2,
-        compiler_params=pltpu.CompilerParams(
-            collective_id=collective_id, has_side_effects=True, vmem_limit_bytes=16 * 2**20
-        ),
-    )(a, b, gain)
-
-
-def middle_kernel(
-    dims,
-    secs,
-    gram_ref,
-    proj_ref,
-    e_ref,
-    c_ref,
-    gall_ref,
-    pall_ref,
-    et_ref,
-    ct_ref,
-    e2_ref,
-    landing,
-    total_ref,
-    send1,
-    recv1,
-    send2,
-    recv2,
-    local_sem,
-    across_send,
-    across_recv,
-    xsend,
-    xrecv,
-    *sems,
-):
-    ring = Ring(dims)
-    count, width = secs[0] * secs[1], secs[1]
-    me = lax.axis_index("section")
-    y0, x0 = me // width, lax.rem(me, width)
-    peers = [{"section": lax.rem(me + j, count)} for j in range(1, count)]
-    across = {"section": (1 - y0) * width + x0}
-    beside = [{"section": y0 * width + lax.rem(x0 + j, width)} for j in range(1, width)]
-    entry = Entry(ring.peers + peers)
-    entry.wait()
+    first.landed()
+    work.project(proj_ref)
     sent = []
 
     def push(*what):
@@ -355,80 +419,90 @@
         copy.start()
         sent.append(copy)
 
-    for j in range(1, count):
-        push(gram_ref.at[lax.rem(me + j, count)], landing.at[me], send1.at[j], recv1.at[j], peers[j - 1])
-    cols, tokens = et_ref.shape
-    odd = 64 if cols % 128 else 0
-    begin = me * cols
-    shift = begin - begin // 128 * 128
-    window = pl.ds(pl.multiple_of(begin // 128 * 128, 128), cols + odd)
-    pick = eye(cols, cols + odd, shift)
-    et_ref[...] = dot_nt(pick, e_ref[:, window]).astype(BF)
-    ct_ref[...] = dot_nt(pick, c_ref[:, window]).astype(BF)
-    square = jnp.zeros((tokens, 128), F32)
-    for i in range(e_ref.shape[1] // 128):
-        piece = e_ref[:, i * 128 : (i + 1) * 128].astype(F32)
-        square = square + piece * piece
-    e2_ref[...] = jnp.broadcast_to(jnp.sum(square, axis=1, keepdims=True), (tokens, 128))
-    total = gram_ref[me].astype(F32)
-    for j in range(1, count):
-        source = lax.rem(me + count - j, count)
-        block = landing.at[source]
-        remote(block, block, send1.at[j], recv1.at[j], peers[j - 1]).wait_recv()
-        total = total + landing[source].astype(F32)
-    total_ref[me] = total.astype(total_ref.dtype)
-    for j in range(1, count):
-        push(total_ref.at[me], total_ref.at[me], send2.at[j], recv2.at[j], peers[j - 1])
     own = pltpu.make_async_copy(proj_ref, pall_ref.at[y0, x0], local_sem)
     own.start()
     push(proj_ref, pall_ref.at[y0, x0], across_send, across_recv, across)
     for j in range(1, width):
         push(proj_ref, pall_ref.at[y0, x0], xsend.at[0, j], xrecv.at[0, j], beside[j - 1])
+    for k in range(max(1, last - 1), last + 1):
+        second.step(k)
+    second.landed()
+    save = pltpu.make_async_copy(col_ref, col_out, save_col)
+    save.start()
+    work.gram(gram_ref)
     for j in range(1, count):
-        block = total_ref.at[lax.rem(me + count - j, count)]
-        remote(block, block, send2.at[j], recv2.at[j], peers[j - 1]).wait_recv()
-
-    def forward():
-        block = pall_ref.at[1 - y0, x0]
-        remote(block, block, across_send, across_recv, across).wait_recv()
-        for j in range(1, width):
-            push(block, block, xsend.at[1, j], xrecv.at[1, j], beside[j - 1])
-
-    Spread(ring, total_ref, gall_ref, sems).run(forward)
+        push(gram_ref, landing.at[me], gsend.at[j], grecv.at[j], peers[j - 1])
+    landing[me] = gram_ref[...]
+    block = pall_ref.at[1 - y0, x0]
+    remote(block, block, across_send, across_recv, across).wait_recv()
+    for j in range(1, width):
+        push(block, block, xsend.at[1, j], xrecv.at[1, j], beside[j - 1])
+    for j in range(1, count):
+        block = landing.at[lax.rem(me + count - j, count)]
+        remote(block, block, gsend.at[j], grecv.at[j], peers[j - 1]).wait_recv()
+    total = landing[0].astype(F32)
+    for i in range(1, count):
+        total = total + landing[i].astype(F32)
+    total_ref[...] = total.astype(BF)
+    third.start()
+    third.first()
+    for k in range(1, last + 1):
+        third.step(k)
     for h in range(2):
         for j in range(1, width):
             landed = pall_ref.at[y0 if h == 0 else 1 - y0, lax.rem(x0 + width - j, width)]
             remote(landed, landed, xsend.at[h, j], xrecv.at[h, j], beside[j - 1]).wait_recv()
+    third.finish()
+    first.drain()
+    second.drain()
     own.wait()
+    save.wait()
+    exchange.wait_send()
     for copy in sent:
         copy.wait_send()
 
 
-def gather_middle(gram, proj, embeds, cotangent, collective_id, dims=DP, secs=SEC):
-    dma = pltpu.SemaphoreType.DMA
+def front(a, b, gain, embeds, cotangent, collective_id, make, dims=DP, secs=SEC, high=64):
+    rows, rank = a.shape
     count = secs[0] * secs[1]
     tokens, width = embeds.shape
+    dma = pltpu.SemaphoreType.DMA
     vmem = pl.BlockSpec(memory_space=pltpu.VMEM)
     anywhere = pl.BlockSpec(memory_space=pl.ANY)
+    tall = rows + high
+    shape = jax.ShapeDtypeStruct
+    own_rows = (rows, high, high, high, rows, tall)
     return pl.pallas_call(
-        functools.partial(middle_kernel, dims, secs),
+        functools.partial(front_kernel, dims, secs, make),
         out_shape=[
-            jax.ShapeDtypeStruct(dims + gram.shape, gram.dtype),
-            jax.ShapeDtypeStruct(secs + proj.shape, proj.dtype),
-            jax.ShapeDtypeStruct((width // count, tokens), BF),
-            jax.ShapeDtypeStruct((width // count, tokens), BF),
-            jax.ShapeDtypeStruct((tokens, 128), F32),
+            shape(dims + (tall, rank), BF),
+            shape(dims + (rank, rank), BF),
+            shape(secs + (tokens, 3 * rank), BF),
+            shape((width // count, tokens), BF),
+            shape((width // count, tokens), BF),
+            shape((tokens, 128), F32),
         ],
-        in_specs=[vmem, anywhere, vmem, vmem],
-        out_specs=[anywhere, anywhere, vmem, vmem, vmem],
-        scratch_shapes=[pltpu.VMEM(gram.shape, gram.dtype)] * 2
-        + [dma((count,))] * 4
-        + [dma, dma, dma, dma((2, secs[1])), dma((2, secs[1]))]
-        + ring_sems(dims),
+        in_specs=[vmem] * 3 + [anywhere] * 2,
+        out_specs=[anywhere] * 3 + [vmem] * 3,
+        scratch_shapes=[pltpu.VMEM((n, rank), BF) for n in own_rows]
+        + [
+            pltpu.VMEM(dims + (rows, rank), BF),
+            pltpu.VMEM(dims + (tall, rank), BF),
+            pltpu.VMEM((tokens, width), BF),
+            pltpu.VMEM((tokens, width), BF),
+            pltpu.VMEM((width, 2 * rank), BF),
+            pltpu.VMEM((tokens, 3 * rank), BF),
+            pltpu.VMEM((rank, rank), BF),
+            pltpu.VMEM((count, rank, rank), BF),
+            pltpu.VMEM((rank, rank), BF),
+        ]
+        + [dma, dma, dma, dma, dma, dma((3,)), dma((3,))]
+        + [dma((count,)), dma((count,)), dma, dma, dma, dma((2, secs[1])), dma((2, secs[1]))]
+        + ring_sems(dims) * 3,
         compiler_params=pltpu.CompilerParams(
-            collective_id=collective_id, has_side_effects=True, vmem_limit_bytes=32 * 2**20
+            collective_id=collective_id, has_side_effects=True, vmem_limit_bytes=48 * 2**20
         ),
-    )(gram, proj, embeds, cotangent)
+    )(a, b, gain, embeds, cotangent)
 
 
 class Scatter:
@@ -539,19 +613,20 @@
 
 def finish_kernel(dims, count, compute, inputs, *refs):
     given, refs = refs[:inputs], refs[inputs:]
-    a_ref, gain_ref, ga_ref, gb_ref, gg_ref, ge_ref, x_ref, mine_low, got_low, mine_high, got_high = refs[:11]
-    low_buffers, high_buffers = refs[11:16], refs[16:21]
-    low_sems, high_sems = refs[21:27], refs[27:33]
-    asems, bsems, gsend, grecv = refs[33:37]
-    ring_part = refs[37:44]
-    scratch = refs[44:]
+    a_ref, gain_ref, ga_ref, gb_ref, gg_ref, ge_ref, x_ref, mine_low, got_low, mine_high = refs[:10]
+    low_buffers, high_buffers = refs[10:15], refs[15:20]
+    low_sems, high_sems = refs[20:26], refs[26:32]
+    asems, gsend, grecv = refs[32:35]
+    ring_part = refs[35:42]
+    scratch = refs[42:]
     ring = Ring(dims)
-    down, up = swap_down(dims, count), swap_up(dims, count)
+    down, gather = swap_down(dims, count), Fan(ring, count, gb_ref, ring_part)
     me = lax.axis_index("section")
     peers = [{"section": lax.rem(me + j, count)} for j in range(1, count)]
-    entry = Entry(ring.peers + peers, (down, up))
+    entry = Entry(ring.peers + peers, (down, gather))
+    entry.count = entry.count + dims[0] - 1
     rows, rank = a_ref.shape
-    high = got_high.shape[0]
+    high = mine_high.shape[0]
     upper = Scatter(ring, x_ref, pl.ds(rows, high), high_buffers, high_sems)
     lower = Scatter(ring, x_ref, pl.ds(0, rows), low_buffers, low_sems)
     work = compute(given, x_ref, ge_ref, scratch)
@@ -570,15 +645,12 @@
     if last > 1:
         lower.step(last - 1)
     mine_high[...] = upper.rows_finish().astype(BF)
-    up.start(mine_high, got_high, bsems)
+    gather.start_from(mine_high)
     lower.step(last)
     lower.rows_start()
     work.rest()
     mine_low[...] = lower.rows_finish().astype(BF)
     down.start(mine_low, got_low, asems)
-    up.wait()
-    gather = Spread(ring, got_high, gb_ref, ring_part)
-    gather.start()
     gather.first()
     down.wait()
     w = got_low[...].astype(F32)
@@ -622,11 +694,11 @@
         in_specs=[vmem] * (len(given) + 2),
         out_specs=[vmem, pl.BlockSpec(memory_space=pl.ANY), vmem, vmem],
         scratch_shapes=[pltpu.VMEM(dims + (rows + high, rank), BF)]
-        + [pltpu.VMEM((n, rank), BF) for n in (rows, rows, high, high)]
+        + [pltpu.VMEM((n, rank), BF) for n in (rows, rows, high)]
         + scatter_buffers(dims, rows, rank)
         + scatter_buffers(dims, high, rank)
         + scatter_sems(dims) * 2
-        + [dma((3,)), dma((3,)), dma((count,)), dma((count,))]
+        + [dma((3,)), dma((count,)), dma((count,))]
         + ring_sems(dims)
         + scratch,
         compiler_params=pltpu.CompilerParams(
@@ -737,8 +809,7 @@
 
 
 def per_device(embeds, cotangent, adapter_a, adapter_b, norm_gains):
-    sec = lax.axis_index("section")
-    dp = lax.axis_index("dp")
+    sec, dp = lax.axis_index("section"), lax.axis_index("dp")
     tokens, width = embeds.shape
     cols = width // CALLS
     a_own = adapter_a[0]
@@ -747,24 +818,8 @@
     gain = jnp.where(sec % 2 == 0, norm_gains[0], norm_gains[1])
     gain_rows = lax.dynamic_slice_in_dim(gain, dp * quarter, quarter, 0)
     gain_rows = jnp.broadcast_to(gain_rows[:, None], (quarter, rank))
-    own, col = gather_weights(a_own, adapter_b[0], gain_rows, 0)
-    own = own.reshape(64, quarter, rank)
+    col, gram, proj, et, ct, e2 = front(a_own, adapter_b[0], gain_rows, embeds, cotangent, 0, Front)
     col = col.reshape(64, quarter + 64, rank)
-    pmat = own[:, :eighth].reshape(2, 32, eighth, rank).transpose(1, 0, 2, 3).reshape(width, rank)
-    up = own[:, eighth:].reshape(width, rank)
-    proj = jnp.concatenate([dot(embeds, jnp.concatenate([pmat, up], axis=1)), dot(cotangent, up)], axis=1)
-
-    lead, spot = dp // 16, dp % 16
-    early = spot < 15 - 2 * lead
-    row = jnp.where(early, lead, CALLS - 1 - lead)
-    pos = jnp.where(early, 2 * lead + spot, spot - 1)
-    other = (pos + 1) // 2
-    bt_of = lambda t: lax.dynamic_slice_in_dim(col, t * 8, 8, 0)[:, quarter : quarter + eighth].reshape(cols, rank)
-    a1 = lax.dynamic_slice_in_dim(col, other * 4, 4, 0)[:, :quarter].reshape(cols, rank)
-    right = jnp.where(pos % 2 == 0, bt_of(other), a1)
-    gpart = lax.dot_general(bt_of(row), right, (((0,), (0,)), ((), ())), preferred_element_type=F32)
-    gpart = gpart.astype(BF).reshape(CALLS, 16, rank)
-    gram, proj, et, ct, e2 = gather_middle(gpart, proj.astype(BF), embeds, cotangent, 1)
     gram = gram.reshape(64, rank, rank)
     proj = proj.reshape(CALLS, tokens, 3 * rank)
 
@@ -777,7 +832,7 @@
         pltpu.VMEM((cols, tokens), F32),
     ]
     grad_a, gb, gains, ge = finish(
-        (proj, e2, gram, et, ct, col), a_own, gain_rows, (cols, tokens), Solver, scratch, 2
+        (proj, e2, gram, et, ct, col), a_own, gain_rows, (cols, tokens), Solver, scratch, 1
     )
     grad_gain = jnp.sum(gains.reshape(CALLS // 2, 2, 8, rank)[:, :, 0, :quarter], axis=0)
     grad_b = gb.reshape(64, 64, rank)[:, :eighth].reshape(width, rank)

time: 166 us -> 160 us (0.964)
  Pallas kernels: 153 us -> 148 us
    pallas_call x2 -> x1, Pallas kernels: 90.6 us -> 83 us  [front(): pl.pallas_call(functools.partial(front_kernel, dims, secs, make), out_sha...]
    pallas_call x1, Pallas kernels: 62.8 us -> 65 us  [finish(): pl.pallas_call(functools.partial(finish_kernel, dims, count, compute, len...]
    unnamed x14 -> x12, local copies, waits for them, and re-layouts: 7.61 us -> 8.95 us
where the time goes in v4:
time: 160 us
  Pallas kernels  148 us (92%)
  local copies, waits for them, and re-layouts  10 us (6%)
    pallas_call x1, Pallas kernels, front(): pl.pallas_call(functools.partial(front_kernel, dims, secs, make), out_sha...  83 us
    pallas_call x1, Pallas kernels, finish(): pl.pallas_call(functools.partial(finish_kernel, dims, count, compute, len...  65 us
    unnamed x12, local copies, waits for them, and re-layouts  8.95 us

profile of v4, /device:TPU:11, one launch (start us, length us, event | category | flops | bytes accessed | tf_op | source)
XLA Modules:
  0.0 159.6 jit_solution(13868208348559383535)
XLA Ops:
  0.6 0.8 copy.12
  1.5 1.0 fusion.1
  2.4 0.1 fusion
  2.5 0.1 broadcast_in_dim.15.refs_2_.refs_7_
  2.6 0.0 copy-start.1
  2.6 1.3 copy-done.1
  3.9 0.0 copy-start.2
  3.9 1.3 copy-done.2
  5.3 0.0 copy-start.3
  5.3 0.7 copy-done.3
  6.0 83.0 %shard_map.84 = (bf16[4,8,2,176,128]{4,3,2,1,0:T(8,128)(2,1)}, bf16[4,8,2,128,128]{4,3,2,1,0:T(8,128)(2,1)}, bf16[2,4,192,384]{3,2,1,0:T(8,128)(2,1)S(1)}, bf16[...) custom-call(bf16[112,128]{1,0:T(8,128)(2,1)S(1)} %bitcast.23, ...), custom_call_target="tpu_custom_call" | custom-call | tf_op jit(solution)/shard_map/pallas_call | solution.py:475
  89.1 0.0 copy-start
  89.1 1.6 copy-done
  90.7 65.0 %shard_map.85 = (f32[112,128]{1,0:T(8,128)S(1)}, bf16[4,8,2,64,128]{4,3,2,1,0:T(8,128)(2,1)S(1)}, f32[8,8,128]{2,1,0:T(8,128)S(1)}, bf16[448,192]{1,0:T(8,128)(2,1)S(1)}) custom-call(bf16[8,192,384]{2,1,0:T(8,128)(2,1)S(1)} %bitcast.19, f32[192,128]{1,0:T(8,128)S(1)} %get-tuple-element.15.refs_1_, bf16[64,128,128]{2,1,0:T(8,128)(2,1)S(1)} %bitcast.18, ...), custom_call_target="tpu_custom_call" | custom-call | tf_op jit(solution)/shard_map/pallas_call | solution.py:686
  155.7 0.1 slice.16
  155.8 0.6 slice_reduce_fusion
  156.3 0.8 copy.14
  157.1 0.2 convert_bitcast_fusion
  157.3 1.7 %copy.13 = f32[1,128,3584]{2,1,0:T(8,128)} copy(f32[1,128,3584]{1,2,0:T(8,128)S(1)} %convert_bitcast_fusion) | data formatting | bytes 3670016
  159.0 0.6 copy.16
Async XLA Ops:
  2.6 1.4 copy-start.1
  3.9 1.3 copy-start.2
  5.3 0.7 copy-start.3
  89.1 1.6 copy-start

commit v5 on v4

--- a/solution.py
+++ b/solution.py
@@ -346,14 +346,132 @@
         out_ref[...] = value.astype(BF)
 
 
-def front_kernel(dims, secs, make, *refs):
-    a_ref, b_ref, gain_ref, e_hbm, c_hbm = refs[:5]
-    col_out, gall_ref, pall_ref, et_ref, ct_ref, e2_ref = refs[5:11]
-    scaled, b_rows, give, other, own_sec, own_col = refs[11:17]
-    sec_ref, col_ref, e_ref, c_ref, wide_ref, proj_ref, gram_ref, landing, total_ref = refs[17:26]
-    load_e, load_c, save_col, hsend, hrecv, asems, bsems = refs[26:33]
-    gsend, grecv, local_sem, across_send, across_recv, xsend, xrecv = refs[33:40]
-    first_sems, second_sems, third_sems = refs[40:47], refs[47:54], refs[54:61]
+class Scatter:
+    def __init__(self, ring, x_ref, rows, buffers, sems):
+        self.ring, self.x, self.rows = ring, x_ref, rows
+        self.from_core, self.moving, self.landing, self.rest, self.from_row = buffers
+        self.sems = sems
+        self.sent = []
+        self.ready = set()
+        self.totals = {}
+
+    def push(self, *what):
+        copy = remote(*what)
+        copy.start()
+        self.sent.append(copy)
+
+    def start(self):
+        ring = self.ring
+        zs = ring.dims[1]
+        csend, crecv = self.sems[:2]
+        for offset in sorted(range(zs), key=lambda o: -min(o, zs - o)):
+            z = lax.rem(ring.z + offset, zs)
+            self.push(
+                self.x.at[:, z, 1 - ring.c, self.rows],
+                self.from_core.at[offset],
+                csend.at[offset],
+                crecv.at[offset],
+                ring.sibling,
+            )
+
+    def need(self, offset):
+        csend, crecv = self.sems[:2]
+        if offset not in self.ready:
+            self.ready.add(offset)
+            block = self.from_core.at[offset]
+            remote(block, block, csend.at[offset], crecv.at[offset], self.ring.sibling).wait_recv()
+
+    def local_sum(self, offset, j):
+        self.need(offset)
+        ring = self.ring
+        z = lax.rem(ring.z + offset, ring.dims[1])
+        return self.x[j, z, ring.c, self.rows].astype(F32) + self.from_core[offset, j].astype(F32)
+
+    def step(self, k):
+        ring = self.ring
+        ys, zs, _ = ring.dims
+        zsend, zrecv = self.sems[2:4]
+        for j in range(ys):
+            for side in range(2):
+                count = hops(zs, j, ys)[side]
+                step = k - (zs // 2 - count)
+                if step < 0:
+                    continue
+                reach = count - step
+                offset = reach if side == 0 else (zs - reach) % zs
+                got = 0.0
+                if step:
+                    spot = (side, j, step - 1)
+                    block = self.landing.at[spot]
+                    remote(block, block, zsend.at[spot], zrecv.at[spot], ring.sides[side]).wait_recv()
+                    got = self.landing[spot].astype(F32)
+                if reach:
+                    spot = (side, j, step)
+                    self.moving[spot] = (self.local_sum(offset, j) + got).astype(BF)
+                    self.push(
+                        self.moving.at[spot], self.landing.at[spot], zsend.at[spot], zrecv.at[spot], ring.sides[side]
+                    )
+                elif j not in self.totals:
+                    self.totals[j] = self.local_sum(0, j) + got
+                else:
+                    self.rest[j] = (self.totals[j] + got).astype(BF)
+
+    def rows_start(self):
+        ring = self.ring
+        ys = ring.dims[0]
+        ysend, yrecv = self.sems[4:6]
+        for i in range(1, ys):
+            row = lax.rem(ring.y + i, ys)
+            self.push(self.rest.at[row], self.from_row.at[i], ysend.at[i], yrecv.at[i], ring.rows[i - 1])
+
+    def rows_finish(self):
+        ring = self.ring
+        ysend, yrecv = self.sems[4:6]
+        own = self.rest[ring.y].astype(F32)
+        for i in range(1, ring.dims[0]):
+            block = self.from_row.at[i]
+            remote(block, block, ysend.at[i], yrecv.at[i], ring.rows[i - 1]).wait_recv()
+            own = own + self.from_row[i].astype(F32)
+        return own
+
+    def finish(self):
+        for copy in self.sent:
+            copy.wait_send()
+
+
+def scatter_buffers(dims, rows, rank):
+    ys, zs, _ = dims
+    block = (rows, rank)
+    shapes = [(zs, ys), (2, ys, zs // 2), (2, ys, zs // 2), (ys,), (ys,)]
+    return [pltpu.VMEM(shape + block, BF) for shape in shapes]
+
+
+def scatter_sems(dims):
+    ys, zs, _ = dims
+    dma = pltpu.SemaphoreType.DMA
+    return [dma((zs,)), dma((zs,)), dma((2, ys, zs // 2)), dma((2, ys, zs // 2)), dma((ys,)), dma((ys,))]
+
+
+def whole_kernel(dims, secs, make, compute, *refs):
+    refs = list(refs)
+
+    def take(n):
+        got = refs[:n]
+        del refs[:n]
+        return got
+
+    a_ref, b_ref, gain_ref, e_hbm, c_hbm = take(5)
+    ga_ref, gb_ref, gg_ref, ge_ref = take(4)
+    scaled, b_rows, give, other, own_sec, own_col = take(6)
+    sec_ref, col_ref, e_ref, c_ref, wide_ref, proj_ref, gram_ref, landing, total_ref = take(9)
+    gall_ref, pall_ref, et_ref, ct_ref, e2_ref = take(5)
+    x_ref, mine_low, got_low, mine_high = take(4)
+    low_buffers, high_buffers = take(5), take(5)
+    load_e, load_c, hsend, hrecv, asems, bsems, csems = take(7)
+    gsend, grecv, tsend, trecv, local_sem, across_send, across_recv, xsend, xrecv = take(9)
+    first_sems, second_sems, third_sems, ring_part = take(7), take(7), take(7), take(7)
+    low_sems, high_sems = take(6), take(6)
+    scratch = refs
     ring = Ring(dims)
     count, width = secs[0] * secs[1], secs[1]
     me = lax.axis_index("section")
@@ -361,8 +479,10 @@
     peers = [{"section": lax.rem(me + j, count)} for j in range(1, count)]
     across = {"section": (1 - y0) * width + x0}
     beside = [{"section": y0 * width + lax.rem(x0 + j, width)} for j in range(1, width)]
-    down, up = swap_down(dims, count), swap_up(dims, count)
-    entry = Entry(ring.peers + peers, (down, up))
+    down, up, back = swap_down(dims, count), swap_up(dims, count), swap_down(dims, count)
+    gather = Fan(ring, count, gb_ref, ring_part)
+    entry = Entry(ring.peers + peers, (down, up, gather))
+    entry.count = entry.count + dims[0] - 1
     loads = [pltpu.make_async_copy(e_hbm, e_ref, load_e), pltpu.make_async_copy(c_hbm, c_ref, load_c)]
     for load in loads:
         load.start()
@@ -396,22 +516,6 @@
     second = Spread(ring, own_col, col_ref, second_sems)
     third = Spread(ring, total_ref, gall_ref, third_sems)
     last = dims[1] // 2
-    first.start()
-    first.first()
-    first.step(1)
-    down.wait()
-    up.wait()
-    second.start()
-    for k in range(2, last + 1):
-        first.step(k)
-        if k == 2:
-            second.first()
-        else:
-            second.step(k - 2)
-    if last < 2:
-        second.first()
-    first.landed()
-    work.project(proj_ref)
     sent = []
 
     def push(*what):
@@ -419,24 +523,29 @@
         copy.start()
         sent.append(copy)
 
+    first.start()
+    first.first()
+    down.wait()
+    up.wait()
+    second.start()
+    first.step(1)
+    second.first()
+    for k in range(1, last + 1):
+        second.step(k)
+        if k < last:
+            first.step(k + 1)
+    second.landed()
+    work.gram(gram_ref)
+    for j in range(1, count):
+        push(gram_ref, landing.at[me], gsend.at[j], grecv.at[j], peers[j - 1])
+    landing[me] = gram_ref[...]
+    first.landed()
+    work.project(proj_ref)
     own = pltpu.make_async_copy(proj_ref, pall_ref.at[y0, x0], local_sem)
     own.start()
     push(proj_ref, pall_ref.at[y0, x0], across_send, across_recv, across)
     for j in range(1, width):
         push(proj_ref, pall_ref.at[y0, x0], xsend.at[0, j], xrecv.at[0, j], beside[j - 1])
-    for k in range(max(1, last - 1), last + 1):
-        second.step(k)
-    second.landed()
-    save = pltpu.make_async_copy(col_ref, col_out, save_col)
-    save.start()
-    work.gram(gram_ref)
-    for j in range(1, count):
-        push(gram_ref, landing.at[me], gsend.at[j], grecv.at[j], peers[j - 1])
-    landing[me] = gram_ref[...]
-    block = pall_ref.at[1 - y0, x0]
-    remote(block, block, across_send, across_recv, across).wait_recv()
-    for j in range(1, width):
-        push(block, block, xsend.at[1, j], xrecv.at[1, j], beside[j - 1])
     for j in range(1, count):
         block = landing.at[lax.rem(me + count - j, count)]
         remote(block, block, gsend.at[j], grecv.at[j], peers[j - 1]).wait_recv()
@@ -446,213 +555,45 @@
     total_ref[...] = total.astype(BF)
     third.start()
     third.first()
-    for k in range(1, last + 1):
+    third.step(1)
+    block = pall_ref.at[1 - y0, x0]
+    remote(block, block, across_send, across_recv, across).wait_recv()
+    for j in range(1, width):
+        push(block, block, xsend.at[1, j], xrecv.at[1, j], beside[j - 1])
+    for k in range(2, last + 1):
         third.step(k)
     for h in range(2):
         for j in range(1, width):
             landed = pall_ref.at[y0 if h == 0 else 1 - y0, lax.rem(x0 + width - j, width)]
             remote(landed, landed, xsend.at[h, j], xrecv.at[h, j], beside[j - 1]).wait_recv()
-    third.finish()
-    first.drain()
-    second.drain()
+    third.landed()
     own.wait()
-    save.wait()
-    exchange.wait_send()
-    for copy in sent:
-        copy.wait_send()
-
-
-def front(a, b, gain, embeds, cotangent, collective_id, make, dims=DP, secs=SEC, high=64):
-    rows, rank = a.shape
-    count = secs[0] * secs[1]
-    tokens, width = embeds.shape
-    dma = pltpu.SemaphoreType.DMA
-    vmem = pl.BlockSpec(memory_space=pltpu.VMEM)
-    anywhere = pl.BlockSpec(memory_space=pl.ANY)
-    tall = rows + high
-    shape = jax.ShapeDtypeStruct
-    own_rows = (rows, high, high, high, rows, tall)
-    return pl.pallas_call(
-        functools.partial(front_kernel, dims, secs, make),
-        out_shape=[
-            shape(dims + (tall, rank), BF),
-            shape(dims + (rank, rank), BF),
-            shape(secs + (tokens, 3 * rank), BF),
-            shape((width // count, tokens), BF),
-            shape((width // count, tokens), BF),
-            shape((tokens, 128), F32),
-        ],
-        in_specs=[vmem] * 3 + [anywhere] * 2,
-        out_specs=[anywhere] * 3 + [vmem] * 3,
-        scratch_shapes=[pltpu.VMEM((n, rank), BF) for n in own_rows]
-        + [
-            pltpu.VMEM(dims + (rows, rank), BF),
-            pltpu.VMEM(dims + (tall, rank), BF),
-            pltpu.VMEM((tokens, width), BF),
-            pltpu.VMEM((tokens, width), BF),
-            pltpu.VMEM((width, 2 * rank), BF),
-            pltpu.VMEM((tokens, 3 * rank), BF),
-            pltpu.VMEM((rank, rank), BF),
-            pltpu.VMEM((count, rank, rank), BF),
-            pltpu.VMEM((rank, rank), BF),
-        ]
-        + [dma, dma, dma, dma, dma, dma((3,)), dma((3,))]
-        + [dma((count,)), dma((count,)), dma, dma, dma, dma((2, secs[1])), dma((2, secs[1]))]
-        + ring_sems(dims) * 3,
-        compiler_params=pltpu.CompilerParams(
-            collective_id=collective_id, has_side_effects=True, vmem_limit_bytes=48 * 2**20
-        ),
-    )(a, b, gain, embeds, cotangent)
-
-
-class Scatter:
-    def __init__(self, ring, x_ref, rows, buffers, sems):
-        self.ring, self.x, self.rows = ring, x_ref, rows
-        self.from_core, self.moving, self.landing, self.rest, self.from_row = buffers
-        self.sems = sems
-        self.sent = []
-        self.ready = set()
-        self.totals = {}
-
-    def push(self, *what):
-        copy = remote(*what)
-        copy.start()
-        self.sent.append(copy)
-
-    def start(self):
-        ring = self.ring
-        zs = ring.dims[1]
-        csend, crecv = self.sems[:2]
-        for offset in sorted(range(zs), key=lambda o: -min(o, zs - o)):
-            z = lax.rem(ring.z + offset, zs)
-            self.push(
-                self.x.at[:, z, 1 - ring.c, self.rows],
-                self.from_core.at[offset],
-                csend.at[offset],
-                crecv.at[offset],
-                ring.sibling,
-            )
-
-    def need(self, offset):
-        csend, crecv = self.sems[:2]
-        if offset not in self.ready:
-            self.ready.add(offset)
-            block = self.from_core.at[offset]
-            remote(block, block, csend.at[offset], crecv.at[offset], self.ring.sibling).wait_recv()
-
-    def local_sum(self, offset, j):
-        self.need(offset)
-        ring = self.ring
-        z = lax.rem(ring.z + offset, ring.dims[1])
-        return self.x[j, z, ring.c, self.rows].astype(F32) + self.from_core[offset, j].astype(F32)
-
-    def step(self, k):
-        ring = self.ring
-        ys, zs, _ = ring.dims
-        zsend, zrecv = self.sems[2:4]
-        for j in range(ys):
-            for side in range(2):
-                count = hops(zs, j, ys)[side]
-                step = k - (zs // 2 - count)
-                if step < 0:
-                    continue
-                reach = count - step
-                offset = reach if side == 0 else (zs - reach) % zs
-                got = 0.0
-                if step:
-                    spot = (side, j, step - 1)
-                    block = self.landing.at[spot]
-                    remote(block, block, zsend.at[spot], zrecv.at[spot], ring.sides[side]).wait_recv()
-                    got = self.landing[spot].astype(F32)
-                if reach:
-                    spot = (side, j, step)
-                    self.moving[spot] = (self.local_sum(offset, j) + got).astype(BF)
-                    self.push(
-                        self.moving.at[spot], self.landing.at[spot], zsend.at[spot], zrecv.at[spot], ring.sides[side]
-                    )
-                elif j not in self.totals:
-                    self.totals[j] = self.local_sum(0, j) + got
-                else:
-                    self.rest[j] = (self.totals[j] + got).astype(BF)
-
-    def rows_start(self):
-        ring = self.ring
-        ys = ring.dims[0]
-        ysend, yrecv = self.sems[4:6]
-        for i in range(1, ys):
-            row = lax.rem(ring.y + i, ys)
-            self.push(self.rest.at[row], self.from_row.at[i], ysend.at[i], yrecv.at[i], ring.rows[i - 1])
-
-    def rows_finish(self):
-        ring = self.ring
-        ysend, yrecv = self.sems[4:6]
-        own = self.rest[ring.y].astype(F32)
-        for i in range(1, ring.dims[0]):
-            block = self.from_row.at[i]
-            remote(block, block, ysend.at[i], yrecv.at[i], ring.rows[i - 1]).wait_recv()
-            own = own + self.from_row[i].astype(F32)
-        return own
-
-    def finish(self):
-        for copy in self.sent:
-            copy.wait_send()
-
-
-def scatter_buffers(dims, rows, rank):
-    ys, zs, _ = dims
-    block = (rows, rank)
-    shapes = [(zs, ys), (2, ys, zs // 2), (2, ys, zs // 2), (ys,), (ys,)]
-    return [pltpu.VMEM(shape + block, BF) for shape in shapes]
-
-
-def scatter_sems(dims):
-    ys, zs, _ = dims
-    dma = pltpu.SemaphoreType.DMA
-    return [dma((zs,)), dma((zs,)), dma((2, ys, zs // 2)), dma((2, ys, zs // 2)), dma((ys,)), dma((ys,))]
-
-
-def finish_kernel(dims, count, compute, inputs, *refs):
-    given, refs = refs[:inputs], refs[inputs:]
-    a_ref, gain_ref, ga_ref, gb_ref, gg_ref, ge_ref, x_ref, mine_low, got_low, mine_high = refs[:10]
-    low_buffers, high_buffers = refs[10:15], refs[15:20]
-    low_sems, high_sems = refs[20:26], refs[26:32]
-    asems, gsend, grecv = refs[32:35]
-    ring_part = refs[35:42]
-    scratch = refs[42:]
-    ring = Ring(dims)
-    down, gather = swap_down(dims, count), Fan(ring, count, gb_ref, ring_part)
-    me = lax.axis_index("section")
-    peers = [{"section": lax.rem(me + j, count)} for j in range(1, count)]
-    entry = Entry(ring.peers + peers, (down, gather))
-    entry.count = entry.count + dims[0] - 1
-    rows, rank = a_ref.shape
-    high = mine_high.shape[0]
-    upper = Scatter(ring, x_ref, pl.ds(rows, high), high_buffers, high_sems)
+    given = (pall_ref, e2_ref, gall_ref, et_ref, ct_ref, col_ref)
+    raised = Scatter(ring, x_ref, pl.ds(rows, high), high_buffers, high_sems)
     lower = Scatter(ring, x_ref, pl.ds(0, rows), low_buffers, low_sems)
-    work = compute(given, x_ref, ge_ref, scratch)
-    work.ups()
-    entry.wait()
-    upper.start()
-    upper.step(0)
-    work.downs()
+    solver = compute(given, x_ref, ge_ref, scratch)
+    solver.ups()
+    raised.start()
+    raised.step(0)
+    solver.downs()
     lower.start()
     last = dims[1] // 2
     for k in range(1, last + 1):
-        upper.step(k)
+        raised.step(k)
         if k > 1 or last == 1:
             lower.step(max(k - 2, 0))
-    upper.rows_start()
+    raised.rows_start()
     if last > 1:
         lower.step(last - 1)
-    mine_high[...] = upper.rows_finish().astype(BF)
+    mine_high[...] = raised.rows_finish().astype(BF)
     gather.start_from(mine_high)
     lower.step(last)
     lower.rows_start()
-    work.rest()
+    solver.rest()
     mine_low[...] = lower.rows_finish().astype(BF)
-    down.start(mine_low, got_low, asems)
+    back.start(mine_low, got_low, csems)
     gather.first()
-    down.wait()
+    back.wait()
     w = got_low[...].astype(F32)
     ga_ref[...] = w * gain_ref[...]
     prod = w * a_ref[...].astype(F32)
@@ -662,9 +603,8 @@
         jnp.ones((8, rank), F32), prod, NT, precision=lax.Precision.HIGHEST, preferred_element_type=F32
     )
     gg_ref[me] = line.astype(BF).astype(F32)
-    sent = []
     for j in range(1, count):
-        copy = remote(gg_ref.at[me], gg_ref.at[me], gsend.at[j], grecv.at[j], peers[j - 1])
+        copy = remote(gg_ref.at[me], gg_ref.at[me], tsend.at[j], trecv.at[j], peers[j - 1])
         copy.start()
         sent.append(copy)
     for k in range(1, last + 1):
@@ -672,39 +612,78 @@
     gather.finish()
     for j in range(1, count):
         block = gg_ref.at[lax.rem(me + count - j, count)]
-        remote(block, block, gsend.at[j], grecv.at[j], peers[j - 1]).wait_recv()
+        remote(block, block, tsend.at[j], trecv.at[j], peers[j - 1]).wait_recv()
     for copy in sent:
         copy.wait_send()
-    upper.finish()
+    raised.finish()
     lower.finish()
-
-
-def finish(given, a, gain, ge_shape, compute, scratch, collective_id, dims=DP, count=CALLS, high=64):
+    first.drain()
+    second.drain()
+    third.drain()
+    exchange.wait_send()
+
+
+def whole(a, b, gain, embeds, cotangent, make, compute, scratch, dims=DP, secs=SEC, high=64):
     rows, rank = a.shape
+    count = secs[0] * secs[1]
+    tokens, width = embeds.shape
+    cols = width // count
     dma = pltpu.SemaphoreType.DMA
     vmem = pl.BlockSpec(memory_space=pltpu.VMEM)
+    anywhere = pl.BlockSpec(memory_space=pl.ANY)
+    tall = rows + high
+    shape = jax.ShapeDtypeStruct
+
+    def buffer(*size, kind=BF):
+        return pltpu.VMEM(size, kind)
+
     return pl.pallas_call(
-        functools.partial(finish_kernel, dims, count, compute, len(given)),
+        functools.partial(whole_kernel, dims, secs, make, compute),
         out_shape=[
-            jax.ShapeDtypeStruct(a.shape, F32),
-            jax.ShapeDtypeStruct(dims + (high, rank), BF),
-            jax.ShapeDtypeStruct((count, 8, rank), F32),
-            jax.ShapeDtypeStruct(ge_shape, BF),
+            shape(a.shape, F32),
+            shape(dims + (high, rank), BF),
+            shape((count, 8, rank), F32),
+            shape((cols, tokens), BF),
         ],
-        in_specs=[vmem] * (len(given) + 2),
-        out_specs=[vmem, pl.BlockSpec(memory_space=pl.ANY), vmem, vmem],
-        scratch_shapes=[pltpu.VMEM(dims + (rows + high, rank), BF)]
-        + [pltpu.VMEM((n, rank), BF) for n in (rows, rows, high)]
+        in_specs=[vmem] * 3 + [anywhere] * 2,
+        out_specs=[vmem, anywhere, vmem, vmem],
+        scratch_shapes=[buffer(n, rank) for n in (rows, high, high, high, rows, tall)]
+        + [
+            buffer(*dims, rows, rank),
+            buffer(*dims, tall, rank),
+            buffer(tokens, width),
+            buffer(tokens, width),
+            buffer(width, 2 * rank),
+            buffer(tokens, 3 * rank),
+            buffer(rank, rank),
+            buffer(count, rank, rank),
+            buffer(rank, rank),
+            buffer(*dims, rank, rank),
+            buffer(*secs, tokens, 3 * rank),
+            buffer(cols, tokens),
+            buffer(cols, tokens),
+            buffer(tokens, 128, kind=F32),
+            buffer(*dims, tall, rank),
+        ]
+        + [buffer(n, rank) for n in (rows, rows, high)]
         + scatter_buffers(dims, rows, rank)
         + scatter_buffers(dims, high, rank)
+        + [dma] * 4
+        + [dma((3,))] * 3
+        + [dma((count,))] * 4
+        + [dma] * 3
+        + [dma((2, secs[1]))] * 2
+        + ring_sems(dims) * 4
         + scatter_sems(dims) * 2
-        + [dma((3,)), dma((count,)), dma((count,))]
-        + ring_sems(dims)
         + scratch,
         compiler_params=pltpu.CompilerParams(
-            collective_id=collective_id, has_side_effects=True, vmem_limit_bytes=48 * 2**20
+            collective_id=0, has_side_effects=True, vmem_limit_bytes=58 * 2**20
         ),
-    )(*given, a, gain)
+    )(a, b, gain, embeds, cotangent)
+
+
+def dp_spot(index):
+    return index // 16, index // 2 % 8, index % 2
 
 
 class Solver:
@@ -716,16 +695,16 @@
     def down_rows(self, half, t):
         quarter = self.h.shape[1] // 4
         first = half * 4 * CALLS + t * 4
-        return jnp.concatenate([self.col[first + j, :quarter] for j in range(4)], axis=0)
+        return jnp.concatenate([self.col[dp_spot(first + j)][:quarter] for j in range(4)], axis=0)
 
     def up_rows(self, t):
         quarter = self.h.shape[1] // 4
         eighth = quarter // 2
-        pieces = [self.col[t * 8 + j, quarter:].astype(F32)[:eighth] for j in range(8)]
+        pieces = [self.col[dp_spot(t * 8 + j)][quarter:].astype(F32)[:eighth] for j in range(8)]
         return jnp.concatenate(pieces, axis=0).astype(BF)
 
     def put(self, index, rows, value):
-        self.x[index // 16, index // 2 % 8, index % 2, rows] = value
+        self.x[(*dp_spot(index), rows)] = value
 
     def ups(self):
         proj_ref, e2_ref, gram_ref, et_ref, ct_ref, _ = self.given
@@ -735,14 +714,14 @@
         scale = 1.0 / (2 * cols * CALLS)
 
         def gram(t, pos):
-            return gram_ref[14 * t + pos if 2 * t < CALLS else 16 * (CALLS - 1 - t) + pos + 1]
+            return gram_ref[dp_spot(14 * t + pos if 2 * t < CALLS else 16 * (CALLS - 1 - t) + pos + 1)]
 
         e2 = e2_ref[:, :1]
         h2 = e2
         invs = []
         for s in range(CALLS):
-            pre = proj_ref[s, :, :rank].astype(F32)
-            hb = proj_ref[s, :, rank : 2 * rank].astype(F32)
+            pre = proj_ref[s // 4, s % 4, :, :rank].astype(F32)
+            hb = proj_ref[s // 4, s % 4, :, rank : 2 * rank].astype(F32)
             for t in range(s):
                 pre = pre + dot(r_ref[t], gram(t, 2 * s - 1))
                 hb = hb + dot(r_ref[t], gram(t, 2 * s))
@@ -758,7 +737,7 @@
         kap = jnp.zeros((tokens, 1), F32)
         kmat = jnp.zeros((tokens, rank), F32)
         for s in reversed(range(CALLS)):
-            u = proj_ref[s, :, 2 * rank :].astype(F32) - kap * hb_ref[s]
+            u = proj_ref[s // 4, s % 4, :, 2 * rank :].astype(F32) - kap * hb_ref[s]
             for t in range(s + 1, CALLS):
                 u = u + dot_nt(v_ref[t], gram(s, 2 * t - 1)) + dot_nt(w_ref[t], gram(s, 2 * t))
             u = u.astype(BF).astype(F32)
@@ -818,11 +797,6 @@
     gain = jnp.where(sec % 2 == 0, norm_gains[0], norm_gains[1])
     gain_rows = lax.dynamic_slice_in_dim(gain, dp * quarter, quarter, 0)
     gain_rows = jnp.broadcast_to(gain_rows[:, None], (quarter, rank))
-    col, gram, proj, et, ct, e2 = front(a_own, adapter_b[0], gain_rows, embeds, cotangent, 0, Front)
-    col = col.reshape(64, quarter + 64, rank)
-    gram = gram.reshape(64, rank, rank)
-    proj = proj.reshape(CALLS, tokens, 3 * rank)
-
     scratch = [
         pltpu.VMEM((CALLS, tokens, rank), BF),
         pltpu.VMEM((CALLS, tokens, rank), BF),
@@ -831,8 +805,8 @@
         pltpu.VMEM((CALLS, cols, tokens), BF),
         pltpu.VMEM((cols, tokens), F32),
     ]
-    grad_a, gb, gains, ge = finish(
-        (proj, e2, gram, et, ct, col), a_own, gain_rows, (cols, tokens), Solver, scratch, 1
+    grad_a, gb, gains, ge = whole(
+        a_own, adapter_b[0], gain_rows, embeds, cotangent, Front, Solver, scratch
     )
     grad_gain = jnp.sum(gains.reshape(CALLS // 2, 2, 8, rank)[:, :, 0, :quarter], axis=0)
     grad_b = gb.reshape(64, 64, rank)[:, :eighth].reshape(width, rank)

time: 160 us -> 159 us (level)
  local copies, waits for them, and re-layouts: 10 us -> 7.5 us
    unnamed x12 -> x8, local copies, waits for them, and re-layouts: 8.95 us -> 4.54 us
    pallas_call x2 -> x1, Pallas kernels: 148 us -> 148 us  [whole(): pl.pallas_call(functools.partial(whole_kernel, dims, secs, make, compute)...]
where the time goes in v5:
time: 159 us; the launch traced here: 158 us
  Pallas kernels  148 us (93%)
  local copies, waits for them, and re-layouts  7.5 us (5%)
  other arithmetic  1.6 us (1%)
    pallas_call x1, Pallas kernels, whole(): pl.pallas_call(functools.partial(whole_kernel, dims, secs, make, compute)...  148 us
    unnamed x8, local copies, waits for them, and re-layouts  4.54 us

profile of v5, /device:TPU:11, one launch (start us, length us, event | category | flops | bytes accessed | tf_op | source)
XLA Modules:
  0.0 158.2 jit_solution(8020135200748247475)
XLA Ops:
  0.6 1.4 copy.12
  2.1 0.9 fusion.1
  3.0 0.1 fusion
  3.1 0.7 broadcast_in_dim.15.refs_2_
  3.8 148.5 %shard_map.84 = (f32[112,128]{1,0:T(8,128)}, bf16[4,8,2,64,128]{4,3,2,1,0:T(8,128)(2,1)}, f32[8,8,128]{2,1,0:T(8,128)}, bf16[448,192]{1,0:T(8,128)(2,1)}) custom-call(bf16[112,128]{1,0:T(8,128)(2,1)} %bitcast.19, bf16[128,56]{1,0:T(8,128)(2,1)} %bitcast.17, f32[112,128]{1,0:T(8,128)} %broadcast_in_dim.15.refs_2_, bf16[192,3584]{1,0:T(8,128)(2,1)} %refs_3_.1, ...), custom_call_target="tpu_custom_call" | custom-call | tf_op jit(solution)/shard_map/pallas_call | solution.py:640
  152.3 0.0 copy-start
  152.3 1.3 slice.16
  153.6 1.3 slice_reduce_fusion
  154.9 0.0 copy-done
  154.9 0.8 copy.14
  155.7 0.2 convert_bitcast_fusion
  155.9 0.0 copy-start.1
  155.9 1.7 %copy.13 = f32[1,128,3584]{2,1,0:T(8,128)} copy(f32[1,128,3584]{1,2,0:T(8,128)S(1)} %convert_bitcast_fusion) | data formatting | bytes 3670016
  157.6 0.0 copy-done.1
  157.6 0.6 copy.16
Async XLA Ops:
  152.3 2.7 %copy-start = (bf16[448,192]{1,0:T(8,128)(2,1)S(1)}, bf16[448,192]{1,0:T(8,128)(2,1)}, u32[]{:S(2)}) copy-start(bf16[448,192]{1,0:T(8,128)(2,1)} %get-tuple-element.11) | copy-start | bytes 516100
  155.9 1.7 %copy-start.1 = (f32[112,128]{1,0:T(8,128)S(1)}, f32[112,128]{1,0:T(8,128)}, u32[]{:S(2)}) copy-start(f32[112,128]{1,0:T(8,128)} %get-tuple-element.8) | copy-start | bytes 172036

commit v6 on v5

--- a/solution.py
+++ b/solution.py
@@ -99,9 +99,6 @@
         for j in range(1, ring.dims[0]):
             self.push(self.src, block, ysend.at[j], yrecv.at[j], ring.rows[j - 1])
 
-    def await_own(self):
-        pass
-
     def relay(self, j, side, k):
         ring = self.ring
         zsend, zrecv = self.sems[3:5]
@@ -124,8 +121,6 @@
             if j:
                 block = self.out.at[self.lines[j], ring.z, ring.c]
                 remote(block, block, ysend.at[j], yrecv.at[j], ring.rows[j - 1]).wait_recv()
-            else:
-                self.await_own()
             for side in range(2):
                 if hops(zs, j, ys)[side]:
                     self.relay(j, side, 0)
@@ -178,6 +173,7 @@
         self.stays = self.call == sec
         self.slot = (slot // (zs * cs), lax.rem(slot // cs, zs), lax.rem(slot, cs))
         self.targets, self.sources = [], []
+        self.far = [ring.at(ring.y, lax.rem(ring.z + o, zs), ring.c) for o in range(2, zs - 1)]
         for i in range(ys):
             y = lax.rem(self.slot[0] + i, ys)
             self.targets.append({"section": self.call, **ring.at(y, *self.slot[1:])})
@@ -185,7 +181,7 @@
             self.sources.append({"section": place // step, "dp": sec * step + lax.rem(place, step)})
 
     def greet(self, sem):
-        for peer in self.sources[1:]:
+        for peer in self.sources[1:] + self.far:
             pl.semaphore_signal(sem, inc=1, device_id=peer, device_id_type=MESH)
 
         @pl.when(jnp.logical_not(self.stays))
@@ -208,6 +204,38 @@
 
         for i in range(1, self.ring.dims[0]):
             self.push(src, spot, ysend.at[i], yrecv.at[i], self.targets[i])
+
+    def spots(self):
+        zs = self.ring.dims[1]
+        half = zs // 2
+        near_first = sorted(range(1, zs), key=lambda o: min(o, zs - o))
+        return [(o, (0, o - 1) if o <= half else (1, o - half - 1)) for o in near_first]
+
+    def first(self):
+        ring = self.ring
+        ys, zs, _ = ring.dims
+        ysend, yrecv, zsend, zrecv = self.sems[1:5]
+        for j in range(ys):
+            block = self.out.at[self.lines[j], ring.z, ring.c]
+            if j:
+                remote(block, block, ysend.at[j], yrecv.at[j], ring.rows[j - 1]).wait_recv()
+            else:
+                self.await_own()
+            for o, (side, k) in reversed(self.spots()):
+                peer = ring.at(ring.y, lax.rem(ring.z + o, zs), ring.c)
+                self.push(block, block, zsend.at[side, j, k], zrecv.at[side, j, k], peer)
+            self.share(j, ring.z, 0)
+
+    def collect(self):
+        ring = self.ring
+        ys, zs, _ = ring.dims
+        zsend, zrecv = self.sems[3:5]
+        for o, (side, k) in self.spots():
+            for j in range(ys):
+                z = lax.rem(ring.z + zs - o, zs)
+                block = self.out.at[self.lines[j], z, ring.c]
+                remote(block, block, zsend.at[side, j, k], zrecv.at[side, j, k], ring.sides[0]).wait_recv()
+                self.share(j, z, zs - o)
 
     def await_own(self):
         ring = self.ring
@@ -461,10 +489,11 @@
         return got
 
     a_ref, b_ref, gain_ref, e_hbm, c_hbm = take(5)
-    ga_ref, gb_ref, gg_ref, ge_ref = take(4)
+    ga_ref, up_ref, gain_out, ge_ref = take(4)
     scaled, b_rows, give, other, own_sec, own_col = take(6)
     sec_ref, col_ref, e_ref, c_ref, wide_ref, proj_ref, gram_ref, landing, total_ref = take(9)
     gall_ref, pall_ref, et_ref, ct_ref, e2_ref = take(5)
+    gb_ref, gg_ref = take(2)
     x_ref, mine_low, got_low, mine_high = take(4)
     low_buffers, high_buffers = take(5), take(5)
     load_e, load_c, hsend, hrecv, asems, bsems, csems = take(7)
@@ -482,7 +511,7 @@
     down, up, back = swap_down(dims, count), swap_up(dims, count), swap_down(dims, count)
     gather = Fan(ring, count, gb_ref, ring_part)
     entry = Entry(ring.peers + peers, (down, up, gather))
-    entry.count = entry.count + dims[0] - 1
+    entry.count = entry.count + dims[0] - 1 + len(gather.far)
     loads = [pltpu.make_async_copy(e_hbm, e_ref, load_e), pltpu.make_async_copy(c_hbm, c_ref, load_c)]
     for load in loads:
         load.start()
@@ -607,12 +636,22 @@
         copy = remote(gg_ref.at[me], gg_ref.at[me], tsend.at[j], trecv.at[j], peers[j - 1])
         copy.start()
         sent.append(copy)
-    for k in range(1, last + 1):
-        gather.step(k)
-    gather.finish()
+    gather.collect()
+    gather.landed()
+    for y in range(dims[0]):
+        pieces = [gb_ref[y, z, c].astype(F32)[:half] for z in range(dims[1]) for c in range(dims[2])]
+        piece = jnp.concatenate(pieces, axis=0).astype(BF)
+        span = piece.shape[0]
+        up_ref[:, y * span : (y + 1) * span] = dot_nt(eye(rank, rank), piece)
     for j in range(1, count):
         block = gg_ref.at[lax.rem(me + count - j, count)]
         remote(block, block, tsend.at[j], trecv.at[j], peers[j - 1]).wait_recv()
+    for parity in range(2):
+        total = gg_ref[parity]
+        for i in range(parity + 2, count, 2):
+            total = total + gg_ref[i]
+        gain_out[parity : parity + 1] = total[:1, :rows]
+    gather.drain()
     for copy in sent:
         copy.wait_send()
     raised.finish()
@@ -641,12 +680,12 @@
         functools.partial(whole_kernel, dims, secs, make, compute),
         out_shape=[
             shape(a.shape, F32),
-            shape(dims + (high, rank), BF),
-            shape((count, 8, rank), F32),
-            shape((cols, tokens), BF),
+            shape((rank, width), F32),
+            shape((2, rows), F32),
+            shape((tokens, cols), BF),
         ],
         in_specs=[vmem] * 3 + [anywhere] * 2,
-        out_specs=[vmem, anywhere, vmem, vmem],
+        out_specs=[vmem] * 4,
         scratch_shapes=[buffer(n, rank) for n in (rows, high, high, high, rows, tall)]
         + [
             buffer(*dims, rows, rank),
@@ -663,6 +702,8 @@
             buffer(cols, tokens),
             buffer(cols, tokens),
             buffer(tokens, 128, kind=F32),
+            buffer(*dims, high, rank),
+            buffer(count, 8, rank, kind=F32),
             buffer(*dims, tall, rank),
         ]
         + [buffer(n, rank) for n in (rows, rows, high)]
@@ -784,7 +825,11 @@
     def rest(self):
         for t in range(CALLS):
             self.acc[...] += dot_nt(self.down_rows(1, t), self.v[t])
-        self.ge[...] = self.acc[...].astype(BF)
+        cols = self.acc.shape[0]
+        turned = lax.dot_general(
+            self.acc[...].astype(BF), eye(cols, cols), (((0,), (0,)), ((), ())), preferred_element_type=F32
+        )
+        self.ge[...] = turned.astype(BF)
 
 
 def per_device(embeds, cotangent, adapter_a, adapter_b, norm_gains):
@@ -805,12 +850,10 @@
         pltpu.VMEM((CALLS, cols, tokens), BF),
         pltpu.VMEM((cols, tokens), F32),
     ]
-    grad_a, gb, gains, ge = whole(
+    grad_a, grad_b, grad_gain, grad_embed = whole(
         a_own, adapter_b[0], gain_rows, embeds, cotangent, Front, Solver, scratch
     )
-    grad_gain = jnp.sum(gains.reshape(CALLS // 2, 2, 8, rank)[:, :, 0, :quarter], axis=0)
-    grad_b = gb.reshape(64, 64, rank)[:, :eighth].reshape(width, rank)
-    return (grad_a[None], grad_b.T.astype(F32)[None], grad_gain, ge.T)
+    return (grad_a[None], grad_b[None], grad_gain, grad_embed)
 
 
 def solution(mesh):

time: 159 us -> 152 us (0.956)
  the two profiles are of different devices: /device:TPU:11 before, /device:TPU:64 now
where the time goes in v6:
time: 152 us
  Pallas kernels  142 us (93%)
  local copies, waits for them, and re-layouts  8.67 us (6%)
    pallas_call x1, Pallas kernels, whole(): pl.pallas_call(functools.partial(whole_kernel, dims, secs, make, compute)...  142 us
    unnamed x9, local copies, waits for them, and re-layouts  7.02 us

profile of v6, /device:TPU:64, one launch (start us, length us, event | category | flops | bytes accessed | tf_op | source)
XLA Modules:
  0.0 151.8 jit_solution(3280347485903265274)
XLA Ops:
  0.6 1.4 copy.9
  2.1 0.9 fusion.1
  3.0 0.1 fusion
  3.1 0.7 broadcast_in_dim.12.refs_2_
  3.8 142.3 %shard_map.84 = (f32[112,128]{1,0:T(8,128)}, f32[128,3584]{1,0:T(8,128)}, f32[2,112]{1,0:T(2,128)}, bf16[192,448]{1,0:T(8,128)(2,1)}) custom-call(bf16[112,128]{1,0:T(8,128)(2,1)} %bitcast.9, bf16[128,56]{1,0:T(8,128)(2,1)} %bitcast.7, f32[112,128]{1,0:T(8,128)} %broadcast_in_dim.12.refs_2_, bf16[192,3584]{1,0:T(8,128)(2,1)} %refs_3_.1, ...), custom_call_target="tpu_custom_call" | custom-call | tf_op jit(solution)/shard_map/pallas_call | solution.py:679
  146.2 1.4 copy.14
  147.6 0.0 copy-start.1
  147.6 0.0 copy-start
  147.6 2.9 %copy.15 = f32[1,128,3584]{2,1,0:T(8,128)} copy(f32[1,128,3584]{2,1,0:T(8,128)} %bitcast.6) | data formatting | bytes 3670016
  150.5 0.0 copy-done.1
  150.5 0.6 copy.16
  151.1 0.0 copy-done
  151.1 0.7 copy.17
Async XLA Ops:
  147.6 2.9 %copy-start.1 = (f32[2,112]{1,0:T(2,128)S(1)}, f32[2,112]{1,0:T(2,128)}, u32[]{:S(2)}) copy-start(f32[2,112]{1,0:T(2,128)} %get-tuple-element.20) | copy-start | bytes 2692
  147.6 3.5 %copy-start = (bf16[192,448]{1,0:T(8,128)(2,1)S(1)}, bf16[192,448]{1,0:T(8,128)(2,1)}, u32[]{:S(2)}) copy-start(bf16[192,448]{1,0:T(8,128)(2,1)} %get-tuple-element.21) | copy-start | bytes 516100
